TPU v7x, 32 devices: a whole 2x2x4 slice. The times are simulated.
32 devices in a mesh: section: 2 (over core), batch: 8 (over z, x), tensor: 2 (over y).
Axes of the slice: x: 2, y: 2, z: 4, core: 2. Of those that a mesh axis runs over, the one named last changes fastest.
Arguments:
- section_ends: bfloat16 [2, 16, 512, 768], P('section', 'batch', 'tensor'), may hold values from -6 to 6
- lengths: int32 [16, 4], P('batch'), may hold values from 1 to 256, 512 in all within a row
- w_query: bfloat16 [2, 768, 768], P('section', None, 'tensor'), may hold values from -0.21875 to 0.21875
- b_query: float32 [2, 768], P('section', 'tensor'), may hold values from -3 to 3
- w_key: bfloat16 [2, 768, 768], P('section', None, 'tensor'), may hold values from -0.21875 to 0.21875
- w_value: bfloat16 [2, 768, 768], P('section', None, 'tensor'), may hold values from -0.21875 to 0.21875
- b_value: float32 [2, 768], P('section', 'tensor'), may hold values from -3 to 3
- w_out: bfloat16 [2, 768, 768], P('section', 'tensor'), may hold values from -0.875 to 0.875
- b_out: float32 [2, 768], P('section'), may hold values from -3 to 3
- norm1_gain: float32 [2, 768], P('section'), may hold values from 0.25 to 1.75
- norm1_bias: float32 [2, 768], P('section'), may hold values from -2 to 2
- w_inner: bfloat16 [2, 768, 3072], P('section', None, 'tensor'), may hold values from -0.21875 to 0.21875
- b_inner: float32 [2, 3072], P('section', 'tensor'), may hold values from -3 to 3
- w_outer: bfloat16 [2, 3072, 768], P('section', 'tensor'), may hold values from -0.109375 to 0.109375
- b_outer: float32 [2, 768], P('section'), may hold values from -3 to 3
- norm2_gain: float32 [2, 768], P('section'), may hold values from 0.25 to 1.75
- norm2_bias: float32 [2, 768], P('section'), may hold values from -2 to 2
Outputs:
- section_results: bfloat16 [2, 16, 512, 768], P('section', 'batch', 'tensor')
- grad_w_query: float32 [2, 768, 768], P('section', None, 'tensor')
- grad_b_query: float32 [2, 768], P('section', 'tensor')
- grad_w_key: float32 [2, 768, 768], P('section', None, 'tensor')
- grad_w_value: float32 [2, 768, 768], P('section', None, 'tensor')
- grad_b_value: float32 [2, 768], P('section', 'tensor')
- grad_w_out: float32 [2, 768, 768], P('section', 'tensor')
- grad_b_out: float32 [2, 768], P('section')
- grad_norm1_gain: float32 [2, 768], P('section')
- grad_norm1_bias: float32 [2, 768], P('section')
- grad_w_inner: float32 [2, 768, 3072], P('section', None, 'tensor')
- grad_b_inner: float32 [2, 3072], P('section', 'tensor')
- grad_w_outer: float32 [2, 3072, 768], P('section', 'tensor')
- grad_b_outer: float32 [2, 768], P('section')
- grad_norm2_gain: float32 [2, 768], P('section')
- grad_norm2_bias: float32 [2, 768], P('section')
Inputs may be any that keep to these rules, and one draw needn't show every extreme that they name: Each row of lengths sums to 512; a slot's sentences fill it in order with no padding, and tokens attend only within their own sentence.
All inputs are finite; a program needn't handle non-finite values.
Results may differ from a plain program's by a relative error of at most 0.025.
Values may be sent and summed in bfloat16 or wider, within the bound.
No kernel may reach another device: no remote copies, remote signals or barrier semaphores. Data moves between devices by JAX's collectives and lax.ppermute only.
A program may use at most 128 MiB of HBM per device.

v0:
```python
import math

import jax
import jax.numpy as jnp
from jax import lax
from jax.sharding import PartitionSpec as P

HD = 64
SLOT = 512
MB = 2


epsilon = 1e-06
root_half = 0.7071067811865476
inverse_root = 0.3989422804014327


def shifted(block, axis, distance):
    devices = range(lax.axis_size(axis))
    route = [(i - distance, i) for i in devices if i - distance in devices]
    return lax.ppermute(block, axis, route)


def segment_ids(length_rows, slot_size):
    bounds = jnp.cumsum(length_rows, axis=1)
    places = jnp.arange(slot_size, dtype=jnp.int32)
    return jnp.sum((places[None, :, None] >= bounds[:, None, :]).astype(jnp.int32), axis=2)


def norm_forward(residue, gain_vector, offset):
    center = residue - jnp.mean(residue, axis=-1, keepdims=True)
    inverse = lax.rsqrt(jnp.mean(center * center, axis=-1, keepdims=True) + epsilon)
    normal_part = center * inverse
    return (normal_part * gain_vector + offset, normal_part, inverse)


def norm_backward(upstream, normal_part, inverse, gain_vector):
    scaled = upstream * gain_vector
    centred = scaled - jnp.mean(scaled, axis=-1, keepdims=True)
    return (
        centred - normal_part * jnp.mean(scaled * normal_part, axis=-1, keepdims=True)
    ) * inverse


def gelu_slope(hidden):
    return (
        0.5 * (1.0 + lax.erf(hidden * root_half))
        + hidden * jnp.exp(-0.5 * hidden * hidden) * inverse_root
    )


def masked_scores(queries, key_rows, segment):
    scale_factor = 1.0 / math.sqrt(queries.shape[-1])
    scores = (
        jnp.einsum("qhd,khd->hqk", queries, key_rows, preferred_element_type=jnp.float32)
        * scale_factor
    )
    same_segment = segment[:, None] == segment[None, :]
    return jnp.where(same_segment[None], scores, -1e30)


def attend_slot(packed):
    queries, key_rows, values, segment = packed
    scores = masked_scores(queries, key_rows, segment)
    highest = jnp.max(scores, axis=-1, keepdims=True)
    raised = jnp.exp(scores - highest)
    totals = jnp.sum(raised, axis=-1, keepdims=True)
    weights_low = (raised / totals).astype(jnp.bfloat16)
    context = jnp.einsum("hqk,khd->qhd", weights_low, values, preferred_element_type=jnp.float32)
    return (context.astype(jnp.bfloat16), (highest + jnp.log(totals))[..., 0])


def attend_back(packed):
    queries, key_rows, values, segment, logsum, grad_context = packed
    scale_factor = 1.0 / math.sqrt(queries.shape[-1])
    probability = jnp.exp(masked_scores(queries, key_rows, segment) - logsum[..., None])
    grad_probs = jnp.einsum(
        "qhd,khd->hqk", grad_context, values, preferred_element_type=jnp.float32
    )
    grad_values = jnp.einsum(
        "hqk,qhd->khd",
        probability.astype(jnp.bfloat16),
        grad_context,
        preferred_element_type=jnp.float32,
    )
    inner_sum = jnp.sum(probability * grad_probs, axis=-1, keepdims=True)
    grad_scores = (probability * (grad_probs - inner_sum)).astype(jnp.bfloat16)
    grad_queries = (
        jnp.einsum("hqk,khd->qhd", grad_scores, key_rows, preferred_element_type=jnp.float32)
        * scale_factor
    )
    grad_keys = (
        jnp.einsum("hqk,qhd->khd", grad_scores, queries, preferred_element_type=jnp.float32)
        * scale_factor
    )
    return (
        grad_queries.astype(jnp.bfloat16),
        grad_keys.astype(jnp.bfloat16),
        grad_values.astype(jnp.bfloat16),
    )


def layer_forward(half_rows, segment, weights):
    (
        w_query,
        b_query,
        w_key,
        w_value,
        b_value,
        w_out,
        b_out,
        gain_one,
        bias_one,
        w_inner,
        b_inner,
        w_outer,
        b_outer,
        gain_two,
        bias_two,
    ) = weights
    full_rows = lax.all_gather(half_rows, "tensor", axis=1, tiled=True)
    slot_count, slot_size, model_width = full_rows.shape
    flat_rows = full_rows.reshape(slot_count * slot_size, model_width)
    queries = (jnp.dot(flat_rows, w_query, preferred_element_type=jnp.float32) + b_query).astype(
        jnp.bfloat16
    )
    key_rows = jnp.dot(flat_rows, w_key, preferred_element_type=jnp.float32).astype(jnp.bfloat16)
    values = (jnp.dot(flat_rows, w_value, preferred_element_type=jnp.float32) + b_value).astype(
        jnp.bfloat16
    )
    local_width = queries.shape[1]
    split_shape = (slot_count, slot_size, local_width // HD, HD)
    context, logsum = lax.map(
        attend_slot,
        (
            queries.reshape(split_shape),
            key_rows.reshape(split_shape),
            values.reshape(split_shape),
            segment,
        ),
    )
    context_flat = context.reshape(slot_count * slot_size, local_width)
    partial_attention = jnp.dot(context_flat, w_out, preferred_element_type=jnp.float32)
    attention = lax.psum_scatter(
        partial_attention.reshape(slot_count, slot_size, model_width),
        "tensor",
        scatter_dimension=1,
        tiled=True,
    )
    residue_one = attention + b_out + half_rows.astype(jnp.float32)
    normed, normal_one, inverse_one = norm_forward(residue_one, gain_one, bias_one)
    ffn_rows = lax.all_gather(normed.astype(jnp.bfloat16), "tensor", axis=1, tiled=True)
    ffn_rows = ffn_rows.reshape(slot_count * slot_size, model_width)
    hidden = jnp.dot(ffn_rows, w_inner, preferred_element_type=jnp.float32) + b_inner
    active = jax.nn.gelu(hidden, approximate=False).astype(jnp.bfloat16)
    partial_ffn = jnp.dot(active, w_outer, preferred_element_type=jnp.float32)
    ffn_total = lax.psum_scatter(
        partial_ffn.reshape(slot_count, slot_size, model_width),
        "tensor",
        scatter_dimension=1,
        tiled=True,
    )
    residue_two = ffn_total + b_outer + normed
    output, normal_two, inverse_two = norm_forward(residue_two, gain_two, bias_two)
    saved_state = (
        flat_rows,
        queries,
        key_rows,
        values,
        context_flat,
        logsum,
        normal_one,
        inverse_one,
        ffn_rows,
        hidden,
        active,
        normal_two,
        inverse_two,
    )
    return (output, saved_state)


def backward_ffn(grad_output, saved_state, weights):
    (
        flat_rows,
        queries,
        key_rows,
        values,
        context_flat,
        logsum,
        normal_one,
        inverse_one,
        ffn_rows,
        hidden,
        active,
        normal_two,
        inverse_two,
    ) = saved_state
    w_inner = weights[9]
    w_outer = weights[11]
    gain_two = weights[13]
    slot_count = grad_output.shape[0]
    model_width = grad_output.shape[2]
    grad_residue_two = norm_backward(grad_output, normal_two, inverse_two, gain_two)
    grad_rows_two = lax.all_gather(
        grad_residue_two.astype(jnp.bfloat16), "tensor", axis=1, tiled=True
    )
    grad_rows_two = grad_rows_two.reshape(-1, model_width)
    grad_w_outer = jnp.einsum(
        "rf,rd->fd", active, grad_rows_two, preferred_element_type=jnp.float32
    )
    grad_active = jnp.einsum(
        "rd,fd->rf", grad_rows_two, w_outer, preferred_element_type=jnp.float32
    )
    grad_hidden = (grad_active * gelu_slope(hidden)).astype(jnp.bfloat16)
    grad_b_inner = jnp.sum(grad_hidden, axis=0, dtype=jnp.float32)
    grad_w_inner = jnp.einsum(
        "rd,rf->df", ffn_rows, grad_hidden, preferred_element_type=jnp.float32
    )
    input_part = jnp.einsum("rf,df->rd", grad_hidden, w_inner, preferred_element_type=jnp.float32)
    grad_normed = (
        lax.psum_scatter(
            input_part.reshape(slot_count, -1, model_width).astype(jnp.bfloat16),
            "tensor",
            scatter_dimension=1,
            tiled=True,
        ).astype(jnp.float32)
        + grad_residue_two
    )
    ffn_parts = (grad_w_inner, grad_b_inner, grad_w_outer)
    ffn_small = (
        jnp.sum(grad_residue_two, axis=(0, 1)),
        jnp.sum(grad_output * normal_two, axis=(0, 1)),
        jnp.sum(grad_output, axis=(0, 1)),
    )
    return (grad_normed, ffn_parts, ffn_small)


def backward_attention(grad_normed, saved_state, weights, segment):
    (
        flat_rows,
        queries,
        key_rows,
        values,
        context_flat,
        logsum,
        normal_one,
        inverse_one,
        ffn_rows,
        hidden,
        active,
        normal_two,
        inverse_two,
    ) = saved_state
    w_query = weights[0]
    w_key = weights[2]
    w_value = weights[3]
    w_out = weights[5]
    gain_one = weights[7]
    slot_count = grad_normed.shape[0]
    model_width = grad_normed.shape[2]
    slot_size = flat_rows.shape[0] // slot_count
    local_width = queries.shape[1]
    split_shape = (slot_count, slot_size, local_width // HD, HD)
    grad_residue_one = norm_backward(grad_normed, normal_one, inverse_one, gain_one)
    grad_rows_one = lax.all_gather(
        grad_residue_one.astype(jnp.bfloat16), "tensor", axis=1, tiled=True
    )
    grad_rows_one = grad_rows_one.reshape(-1, model_width)
    grad_w_out = jnp.einsum(
        "rc,rd->cd", context_flat, grad_rows_one, preferred_element_type=jnp.float32
    )
    grad_context = jnp.einsum("rd,cd->rc", grad_rows_one, w_out, preferred_element_type=jnp.float32)
    grad_context = grad_context.astype(jnp.bfloat16).reshape(split_shape)
    grad_queries, grad_keys, grad_values = lax.map(
        attend_back,
        (
            queries.reshape(split_shape),
            key_rows.reshape(split_shape),
            values.reshape(split_shape),
            segment,
            logsum,
            grad_context,
        ),
    )
    grad_queries = grad_queries.reshape(-1, local_width)
    grad_keys = grad_keys.reshape(-1, local_width)
    grad_values = grad_values.reshape(-1, local_width)
    grad_b_query = jnp.sum(grad_queries, axis=0, dtype=jnp.float32)
    grad_b_value = jnp.sum(grad_values, axis=0, dtype=jnp.float32)
    grad_w_query = jnp.einsum(
        "rd,rc->dc", flat_rows, grad_queries, preferred_element_type=jnp.float32
    )
    grad_w_key = jnp.einsum("rd,rc->dc", flat_rows, grad_keys, preferred_element_type=jnp.float32)
    grad_w_value = jnp.einsum(
        "rd,rc->dc", flat_rows, grad_values, preferred_element_type=jnp.float32
    )
    input_part = (
        jnp.einsum("rc,dc->rd", grad_queries, w_query, preferred_element_type=jnp.float32)
        + jnp.einsum("rc,dc->rd", grad_keys, w_key, preferred_element_type=jnp.float32)
        + jnp.einsum("rc,dc->rd", grad_values, w_value, preferred_element_type=jnp.float32)
    )
    grad_input = (
        lax.psum_scatter(
            input_part.reshape(slot_count, slot_size, model_width).astype(jnp.bfloat16),
            "tensor",
            scatter_dimension=1,
            tiled=True,
        ).astype(jnp.float32)
        + grad_residue_one
    )
    attention_parts = (
        grad_w_query,
        grad_b_query,
        grad_w_key,
        grad_w_value,
        grad_b_value,
        grad_w_out,
    )
    attention_small = (
        jnp.sum(grad_residue_one, axis=(0, 1)),
        jnp.sum(grad_normed * normal_one, axis=(0, 1)),
        jnp.sum(grad_normed, axis=(0, 1)),
    )
    return (grad_input, attention_parts, attention_small)


def shards(
    section_ends,
    lengths,
    w_query,
    b_query,
    w_key,
    w_value,
    b_value,
    w_out,
    b_out,
    norm1_gain,
    norm1_bias,
    w_inner,
    b_inner,
    w_outer,
    b_outer,
    norm2_gain,
    norm2_bias,
):
    weights = tuple(
        (
            member[0]
            for member in (
                w_query,
                b_query,
                w_key,
                w_value,
                b_value,
                w_out,
                b_out,
                norm1_gain,
                norm1_bias,
                w_inner,
                b_inner,
                w_outer,
                b_outer,
                norm2_gain,
                norm2_bias,
            )
        )
    )
    section_index = lax.axis_index("section")
    first_section = section_index == 0
    held_rows = section_ends[0]
    per_batch = held_rows.shape[0] // MB
    segments = segment_ids(lengths, SLOT)
    incoming = jnp.zeros_like(held_rows[:per_batch])
    kept_states = []
    layer_outputs = []
    for tick_index in range(MB + 1):
        micro_index = jnp.clip(tick_index - section_index, 0, MB - 1)
        own_rows = lax.dynamic_slice_in_dim(held_rows, micro_index * per_batch, per_batch, 0)
        layer_in = jnp.where(first_section, own_rows, incoming)
        segment = lax.dynamic_slice_in_dim(segments, micro_index * per_batch, per_batch, 0)
        output, saved_state = layer_forward(layer_in, segment, weights)
        kept_states.append((layer_in, segment))
        layer_outputs.append(output)
        if tick_index < MB:
            incoming = shifted(output.astype(jnp.bfloat16), "section", 1)
    attention_acc = tuple(
        (
            jnp.zeros(member.shape, jnp.float32)
            for member in (weights[0], weights[1], weights[2], weights[3], weights[4], weights[5])
        )
    )
    ffn_acc = tuple(
        (jnp.zeros(member.shape, jnp.float32) for member in (weights[9], weights[10], weights[11]))
    )
    small_acc = tuple(
        (
            jnp.zeros(member.shape, jnp.float32)
            for member in (
                weights[6],
                weights[7],
                weights[8],
                weights[12],
                weights[13],
                weights[14],
            )
        )
    )
    grad_incoming = jnp.zeros_like(held_rows[:per_batch])
    input_grads = []
    for back_index in range(MB + 1):
        micro_index = MB - back_index - section_index
        live_weight = ((micro_index >= 0) & (micro_index < MB)).astype(jnp.float32)
        clipped = jnp.clip(micro_index, 0, MB - 1)
        cotangent = lax.dynamic_slice_in_dim(held_rows, clipped * per_batch, per_batch, 0)
        grad_output = jnp.where(first_section, grad_incoming, cotangent).astype(jnp.float32)
        state_entry = kept_states[MB - back_index]
        segment = state_entry[1]
        saved_state = layer_forward(state_entry[0], segment, weights)[1]
        grad_normed, ffn_parts, ffn_small = backward_ffn(grad_output, saved_state, weights)
        ffn_acc = tuple(
            (running + live_weight * contrib for running, contrib in zip(ffn_acc, ffn_parts))
        )
        grad_input, attention_parts, attention_small = backward_attention(
            grad_normed, saved_state, weights, segment
        )
        attention_acc = tuple(
            (
                running + live_weight * contrib
                for running, contrib in zip(attention_acc, attention_parts)
            )
        )
        small_acc = tuple(
            (
                running + live_weight * contrib
                for running, contrib in zip(small_acc, attention_small + ffn_small)
            )
        )
        input_grads.append(grad_input)
        if back_index < MB:
            grad_incoming = shifted(grad_input.astype(jnp.bfloat16), "section", -1)
    dense_sums = lax.psum(
        (
            attention_acc[0],
            attention_acc[1],
            attention_acc[2],
            attention_acc[3],
            attention_acc[4],
            attention_acc[5],
            ffn_acc[0],
            ffn_acc[1],
            ffn_acc[2],
        ),
        "batch",
    )
    attention_done = dense_sums[:6]
    ffn_done = dense_sums[6:]
    small_done = lax.psum(
        (small_acc[0], small_acc[1], small_acc[2], small_acc[3], small_acc[4], small_acc[5]),
        ("batch", "tensor"),
    )
    pieces = []
    for micro_number in range(MB):
        pieces.append(
            jnp.where(
                first_section, input_grads[MB - micro_number], layer_outputs[micro_number + 1]
            ).astype(jnp.bfloat16)
        )
    section_results = jnp.concatenate(pieces, axis=0)[None]
    return (
        section_results,
        attention_done[0][None],
        attention_done[1][None],
        attention_done[2][None],
        attention_done[3][None],
        attention_done[4][None],
        attention_done[5][None],
        small_done[0][None],
        small_done[1][None],
        small_done[2][None],
        ffn_done[0][None],
        ffn_done[1][None],
        ffn_done[2][None],
        small_done[3][None],
        small_done[4][None],
        small_done[5][None],
    )


def solution(mesh):
    in_specs = (
        P("section", "batch", "tensor", None),
        P("batch", None),
        P("section", None, "tensor"),
        P("section", "tensor"),
        P("section", None, "tensor"),
        P("section", None, "tensor"),
        P("section", "tensor"),
        P("section", "tensor", None),
        P("section", None),
        P("section", None),
        P("section", None),
        P("section", None, "tensor"),
        P("section", "tensor"),
        P("section", "tensor", None),
        P("section", None),
        P("section", None),
        P("section", None),
    )
    out_specs = (
        P("section", "batch", "tensor", None),
        P("section", None, "tensor"),
        P("section", "tensor"),
        P("section", None, "tensor"),
        P("section", None, "tensor"),
        P("section", "tensor"),
        P("section", "tensor", None),
        P("section", None),
        P("section", None),
        P("section", None),
        P("section", None, "tensor"),
        P("section", "tensor"),
        P("section", "tensor", None),
        P("section", None),
        P("section", None),
        P("section", None),
    )
    return jax.shard_map(shards, mesh=mesh, in_specs=in_specs, out_specs=out_specs, check_vma=False)
```

profile of v0, /device:TPU:11, one launch (start us, length us, event | category | flops | bytes accessed | tf_op | source)
XLA Modules:
  0.0 1078.5 jit_solution(5121712174584833701)
XLA Ops:
  8.4 10.7 all_gather.42
  33.5 28.0 %reduce-scatter.13.cloned.1.call-done = f32[1,256,768]{2,1,0:T(8,128)} async-done(((f32[1,512,768]{2,1,0:T(8,128)}), f32[1,256,768]{2,1,0:T(8,128)}) %reduce-scatter.13.cloned.1.call-update) | async-done | bytes 786448 | tf_op jit(solution)/shard_map/reduce_scatter | solution.py:144
  63.5 10.7 all_gather.43
  74.1 9.6 fusion.8
  84.9 2.5 fusion.81
  87.7 27.0 %reduce-scatter.15.cloned.1.call-done = f32[1,256,768]{2,1,0:T(8,128)} async-done(((f32[1,512,768]{2,1,0:T(8,128)}), f32[1,256,768]{2,1,0:T(8,128)}) %reduce-scatter.15.cloned.1.call-update) | async-done | bytes 786448 | tf_op jit(solution)/shard_map/reduce_scatter | solution.py:157
  120.4 11.4 %all_gather.44 = bf16[1,512,768]{2,1,0:T(8,128)(2,1)S(1)} all-gather(bf16[1,256,768]{2,1,0:T(8,128)(2,1)S(1)} %bitcast_select_fusion.3), channel_id=1, replica_groups=mesh['section'=2,'batch'=8,'tensor'=2] {'tensor'}, dimensions={1}, use_global_device_ids=true | all-gather | bytes 1179648 | tf_op jit(solution)/shard_map/all_gather | solution.py:121
  141.1 26.4 %reduce-scatter.17.cloned.1.call-done = f32[1,256,768]{2,1,0:T(8,128)} async-done(((f32[1,512,768]{2,1,0:T(8,128)}), f32[1,256,768]{2,1,0:T(8,128)}) %reduce-scatter.17.cloned.1.call-update) | async-done | bytes 786448 | tf_op jit(solution)/shard_map/reduce_scatter | solution.py:144
  169.4 10.7 all_gather.45
  180.0 10.4 fusion.11
  191.6 2.5 fusion.84
  194.2 27.1 %reduce-scatter.19.cloned.1.call-done = f32[1,256,768]{2,1,0:T(8,128)} async-done(((f32[1,512,768]{2,1,0:T(8,128)}), f32[1,256,768]{2,1,0:T(8,128)}) %reduce-scatter.19.cloned.1.call-update) | async-done | bytes 786448 | tf_op jit(solution)/shard_map/reduce_scatter | solution.py:157
  228.1 11.5 %all_gather.46 = bf16[1,512,768]{2,1,0:T(8,128)(2,1)S(1)} all-gather(bf16[1,256,768]{2,1,0:T(8,128)(2,1)S(1)} %bitcast_select_fusion.1), channel_id=1, replica_groups=mesh['section'=2,'batch'=8,'tensor'=2] {'tensor'}, dimensions={1}, use_global_device_ids=true | all-gather | bytes 1179648 | tf_op jit(solution)/shard_map/all_gather | solution.py:121
  250.2 26.5 %reduce-scatter.21.cloned.1.call-done = f32[1,256,768]{2,1,0:T(8,128)} async-done(((f32[1,512,768]{2,1,0:T(8,128)}), f32[1,256,768]{2,1,0:T(8,128)}) %reduce-scatter.21.cloned.1.call-update) | async-done | bytes 786448 | tf_op jit(solution)/shard_map/reduce_scatter | solution.py:144
  279.1 10.7 all_gather.47
  289.7 9.5 fusion.14
  300.4 2.5 fusion.87
  303.0 27.1 %reduce-scatter.23.cloned.1.call-done = f32[1,256,768]{2,1,0:T(8,128)} async-done(((f32[1,512,768]{2,1,0:T(8,128)}), f32[1,256,768]{2,1,0:T(8,128)}) %reduce-scatter.23.cloned.1.call-update) | async-done | bytes 786448 | tf_op jit(solution)/shard_map/reduce_scatter | solution.py:157
  334.3 10.6 all_gather.48
  344.9 2.8 convert_reduce_fusion.2
  348.9 2.3 fusion.117
  351.7 18.0 %reduce-scatter.25.cloned.1.call-done = bf16[1,256,768]{2,1,0:T(8,128)(2,1)} async-done(((bf16[1,512,768]{2,1,0:T(8,128)(2,1)}), bf16[1,256,768]{2,1,0:T(8,128)(2,1)}) %reduce-scatter.25.cloned.1.call-update) | async-done | bytes 393232 | tf_op jit(solution)/shard_map/reduce_scatter | solution.py:222
  369.7 2.6 multiply_reduce_fusion.5
  372.3 2.4 fusion.246
  374.8 10.7 all_gather.49
  386.3 4.3 multiply_reduce_fusion.2
  392.9 2.1 fusion.130
  400.9 18.4 %reduce-scatter.27.cloned.1.call-done = bf16[1,256,768]{2,1,0:T(8,128)(2,1)} async-done(((bf16[1,512,768]{2,1,0:T(8,128)(2,1)}), bf16[1,256,768]{2,1,0:T(8,128)(2,1)}) %reduce-scatter.27.cloned.1.call-update) | async-done | bytes 393232 | tf_op jit(solution)/shard_map/reduce_scatter | solution.py:304
  420.7 2.9 collective-permute-start.2
  428.1 11.0 %all_gather.50 = bf16[1,512,768]{2,1,0:T(8,128)(2,1)S(1)} all-gather(bf16[1,256,768]{2,1,0:T(8,128)(2,1)S(1)} %get-tuple-element.264), channel_id=1, replica_groups=mesh['section'=2,'batch'=8,'tensor'=2] {'tensor'}, dimensions={1}, use_global_device_ids=true | all-gather | bytes 1179648 | tf_op jit(solution)/shard_map/all_gather | solution.py:205
  439.1 2.8 convert_reduce_fusion.1
  443.1 2.3 fusion.114
  446.3 5.3 fusion.179
  451.6 3.6 fusion.182
  455.3 8.3 reduce-scatter.29.cloned.1.call-done
  463.5 2.6 multiply_reduce_fusion.4
  466.1 2.4 fusion.247
  468.6 10.6 all_gather.51
  480.1 4.4 multiply_reduce_fusion.1
  495.9 5.3 fusion.174
  501.2 3.6 fusion.191
  508.0 4.4 reduce-scatter.31.cloned.1.call-done
  512.3 2.7 fusion.242
  515.0 2.7 collective-permute-start.3
  517.8 2.6 convolution_multiply_fusion.10
  524.2 11.4 %all_gather.52 = bf16[1,512,768]{2,1,0:T(8,128)(2,1)S(1)} all-gather(bf16[1,256,768]{2,1,0:T(8,128)(2,1)S(1)} %get-tuple-element.261), channel_id=1, replica_groups=mesh['section'=2,'batch'=8,'tensor'=2] {'tensor'}, dimensions={1}, use_global_device_ids=true | all-gather | bytes 1179648 | tf_op jit(solution)/shard_map/all_gather | solution.py:205
  535.7 2.8 convert_reduce_fusion
  539.7 2.3 fusion.111
  544.1 3.0 fusion.107
  548.7 7.6 add_bitcast_fusion
  556.3 3.1 reduce-scatter.33.cloned.1.call-done
  559.4 2.6 multiply_reduce_fusion.3
  562.0 2.4 fusion.248
  564.4 10.9 %all_gather.53 = bf16[1,512,768]{2,1,0:T(8,128)(2,1)S(1)} all-gather(bf16[1,256,768]{2,1,0:T(8,128)(2,1)S(1)} %convert_element_type.466), channel_id=1, replica_groups=mesh['section'=2,'batch'=8,'tensor'=2] {'tensor'}, dimensions={1}, use_global_device_ids=true | all-gather | bytes 1179648 | tf_op jit(solution)/shard_map/all_gather | solution.py:266
  576.2 4.7 convert_reduce_fusion.6
  580.9 4.3 multiply_reduce_fusion
  587.2 2.4 convert_reduce_fusion.9
  593.6 8.4 add_bitcast_fusion.1
  621.6 15.6 %all-reduce.1 = (f32[1,384]{1,0:T(1,128)}, f32[1,384]{1,0:T(1,128)}, f32[1,1536]{1,0:T(1,128)}) all-reduce(f32[1,384]{1,0:T(1,128)} %broadcast_in_dim.295, f32[1,384]{1,0:T(1,128)} %broadcast_in_dim.298, f32[1,1536]{1,0:T(1,128)} %broadcast_in_dim.304), channel_id=1, replica_groups=mesh['section'=2,'batch'=8,'tensor'=2] {'batch'}, use_global_device_ids=true, to_apply=%region_51.52 | all-reduce | flops 2304 | bytes 18432 | tf_op jit(solution)/shard_map/psum | solution.py:442
  637.2 65.7 %all-reduce = (f32[1,768]{1,0:T(1,128)}, f32[1,768]{1,0:T(1,128)}, f32[1,768]{1,0:T(1,128)}, f32[1,768]{1,0:T(1,128)}, f32[1,768]{1,0:T(1,128)}, /*index=5*/f32[1,768]{1,0:T(1,128)}) all-reduce(f32[1,768]{1,0:T(1,128)} %broadcast_in_dim.300, ...), channel_id=1, replica_groups=mesh['section'=2,'batch'=8,'tensor'=2] {'batch','tensor'}, use_global_device_ids=true, to_apply=%region_62.63 | all-reduce | flops 4608 | bytes 36864 | tf_op jit(solution)/shard_map/psum | solution.py:458
  705.4 355.3 %all-reduce.5.cloned.1.call-done = (f32[1,768,384]{2,1,0:T(8,128)}, f32[1,768,384]{2,1,0:T(8,128)}, f32[1,768,384]{2,1,0:T(8,128)}, f32[1,384,768]{2,1,0:T(8,128...) async-done(((f32[1,768,384]{2,1,0:T(8,128)}, f32[1,768,384]{2,1,0:T(8,128)}, f32[1,768,384]{2,1,0:T(8,128)}, f32[1,384,768]{2,1,0:T(8,128)}, f32[1,768,1536]{2,1,0:T(8,128)}, ...) | async-done | bytes 14155792 | tf_op jit(solution)/shard_map/psum | solution.py:442
  1060.8 2.5 copy.75
  1066.9 2.2 copy.79
  1069.4 2.2 copy.80
  (549 shorter events, 136.2 us)
Async XLA Ops:
  7.2 66.9 %copy-start = (bf16[1,768,1536]{2,1,0:T(8,128)(2,1)S(1)}, bf16[1,768,1536]{2,1,0:T(8,128)(2,1)}, u32[]{:S(2)}) copy-start(bf16[1,768,1536]{2,1,0:T(8,128)(2,1)} %param.28) | copy-start | bytes 7077892
  7.2 54.3 %reduce-scatter.13.cloned.1.call-start = ((), (), s32[]{:S(2)}) async-start(), calls=%async_computation.12 | async-start | bytes 2359296 | tf_op jit(solution)/shard_map/reduce_scatter | solution.py:144
  33.3 81.3 %reduce-scatter.15.cloned.1.call-start = ((), (), s32[]{:S(2)}) async-start(), calls=%async_computation.13 | async-start | bytes 2359296 | tf_op jit(solution)/shard_map/reduce_scatter | solution.py:157
  33.4 50.3 %copy-start.123 = (f32[768]{0:T(1024)}, f32[768]{0:T(1024)S(1)}, u32[]{:S(2)}) copy-start(f32[768]{0:T(1024)S(1)} %reduce.32) | copy-start | bytes 9220
  33.5 50.2 %copy-start.153 = (f32[1536]{0:T(1024)}, f32[1536]{0:T(1024)S(1)}, u32[]{:S(2)}) copy-start(f32[1536]{0:T(1024)S(1)} %reduce.35) | copy-start | bytes 18436
  63.0 51.7 %copy-start.4 = (f32[1,256,768]{2,1,0:T(8,128)}, f32[1,256,768]{2,1,0:T(8,128)S(1)}, u32[]{:S(2)}) copy-start(f32[1,256,768]{2,1,0:T(8,128)S(1)} %get-tuple-element.290) | copy-start | bytes 2359300
  63.0 51.6 %copy-start.135 = (f32[256]{0:T(256)}, f32[256]{0:T(256)S(1)}, u32[]{:S(2)}) copy-start(f32[256]{0:T(256)S(1)} %broadcast_multiply_fusion.17) | copy-start | bytes 3076
  63.2 51.4 %copy-start.142 = (f32[256]{0:T(256)}, f32[256]{0:T(256)S(1)}, u32[]{:S(2)}) copy-start(f32[256]{0:T(256)S(1)} %add_rsqrt_fusion.5) | copy-start | bytes 3076
  87.5 80.1 %reduce-scatter.17.cloned.1.call-start = ((), (), s32[]{:S(2)}) async-start(), calls=%async_computation.14 | async-start | bytes 2359296 | tf_op jit(solution)/shard_map/reduce_scatter | solution.py:144
  87.6 30.7 %copy-start.124 = (f32[768]{0:T(1024)}, f32[768]{0:T(1024)S(1)}, u32[]{:S(2)}) copy-start(f32[768]{0:T(1024)S(1)} %reduce.36) | copy-start | bytes 9220
  114.6 17.2 %copy-start.41 = (bf16[1,768,384]{2,1,0:T(8,128)(2,1)S(1)}, bf16[1,768,384]{2,1,0:T(8,128)(2,1)}, u32[]{:S(2)}) copy-start(bf16[1,768,384]{2,1,0:T(8,128)(2,1)} %param.19) | copy-start | bytes 1769476
  114.7 17.2 %copy-start.166 = (f32[384]{0:T(512)S(1)}, f32[384]{0:T(512)}, u32[]{:S(2)}) copy-start(f32[384]{0:T(512)} %copy-done.165) | copy-start | bytes 4612
  116.2 16.1 %copy-start.7 = (f32[1,256,768]{2,1,0:T(8,128)}, f32[1,256,768]{2,1,0:T(8,128)S(1)}, u32[]{:S(2)}) copy-start(f32[1,256,768]{2,1,0:T(8,128)S(1)} %get-tuple-element.288) | copy-start | bytes 2359300
  116.5 15.9 %copy-start.36 = (bf16[1,768,384]{2,1,0:T(8,128)(2,1)S(1)}, bf16[1,768,384]{2,1,0:T(8,128)(2,1)}, u32[]{:S(2)}) copy-start(bf16[1,768,384]{2,1,0:T(8,128)(2,1)} %param.21) | copy-start | bytes 1769476
  116.7 3.6 collective-permute-start
  118.3 14.6 %copy-start.25 = (bf16[1,768,384]{2,1,0:T(8,128)(2,1)S(1)}, bf16[1,768,384]{2,1,0:T(8,128)(2,1)}, u32[]{:S(2)}) copy-start(bf16[1,768,384]{2,1,0:T(8,128)(2,1)} %param.22) | copy-start | bytes 1769476
  118.3 14.6 %copy-start.163 = (f32[384]{0:T(512)S(1)}, f32[384]{0:T(512)}, u32[]{:S(2)}) copy-start(f32[384]{0:T(512)} %copy-done.162) | copy-start | bytes 4612
  141.1 80.1 %reduce-scatter.19.cloned.1.call-start = ((), (), s32[]{:S(2)}) async-start(), calls=%async_computation.15 | async-start | bytes 2359296 | tf_op jit(solution)/shard_map/reduce_scatter | solution.py:157
  168.9 21.5 %copy-start.5 = (f32[1,256,768]{2,1,0:T(8,128)}, f32[1,256,768]{2,1,0:T(8,128)S(1)}, u32[]{:S(2)}) copy-start(f32[1,256,768]{2,1,0:T(8,128)S(1)} %get-tuple-element.286) | copy-start | bytes 2359300
  168.9 52.3 %copy-start.137 = (f32[256]{0:T(256)}, f32[256]{0:T(256)S(1)}, u32[]{:S(2)}) copy-start(f32[256]{0:T(256)S(1)} %broadcast_multiply_fusion.15) | copy-start | bytes 3076
  169.2 52.1 %copy-start.146 = (f32[256]{0:T(256)}, f32[256]{0:T(256)S(1)}, u32[]{:S(2)}) copy-start(f32[256]{0:T(256)S(1)} %add_rsqrt_fusion.3) | copy-start | bytes 3076
  180.0 11.5 %copy-start.168 = (bf16[1,1536,768]{2,1,0:T(8,128)(2,1)S(1)}, bf16[1,1536,768]{2,1,0:T(8,128)(2,1)}, u32[]{:S(2)}) copy-start(bf16[1,1536,768]{2,1,0:T(8,128)(2,1)} %param.30) | copy-start | bytes 7077892
  191.6 29.7 %copy-start.125 = (f32[768]{0:T(1024)S(1)}, f32[768]{0:T(1024)}, u32[]{:S(2)}) copy-start(f32[768]{0:T(1024)} %copy-done.124) | copy-start | bytes 9220
  194.1 30.6 %copy-start.149 = (s32[1,512]{1,0:T(1,128)S(1)}, s32[1,512]{1,0:T(1,128)}, u32[]{:S(2)}) copy-start(s32[1,512]{1,0:T(1,128)} %get-tuple-element.293) | copy-start | bytes 6148
  194.1 82.5 %reduce-scatter.21.cloned.1.call-start = ((), (), s32[]{:S(2)}) async-start(), calls=%async_computation.16 | async-start | bytes 2359296 | tf_op jit(solution)/shard_map/reduce_scatter | solution.py:144
  223.2 18.3 %copy-start.37 = (bf16[1,768,384]{2,1,0:T(8,128)(2,1)S(1)}, bf16[1,768,384]{2,1,0:T(8,128)(2,1)}, u32[]{:S(2)}) copy-start(bf16[1,768,384]{2,1,0:T(8,128)(2,1)} %param.21) | copy-start | bytes 1769476
  223.4 3.6 collective-permute-start.1
  224.9 17.0 %copy-start.26 = (bf16[1,768,384]{2,1,0:T(8,128)(2,1)S(1)}, bf16[1,768,384]{2,1,0:T(8,128)(2,1)}, u32[]{:S(2)}) copy-start(bf16[1,768,384]{2,1,0:T(8,128)(2,1)} %param.22) | copy-start | bytes 1769476
  225.0 17.0 %copy-start.164 = (f32[384]{0:T(512)S(1)}, f32[384]{0:T(512)}, u32[]{:S(2)}) copy-start(f32[384]{0:T(512)} %copy-done.162) | copy-start | bytes 4612
  250.1 79.9 %reduce-scatter.23.cloned.1.call-start = ((), (), s32[]{:S(2)}) async-start(), calls=%async_computation.17 | async-start | bytes 2359296 | tf_op jit(solution)/shard_map/reduce_scatter | solution.py:157
  276.7 13.1 %copy-start.154 = (f32[1536]{0:T(1024)S(1)}, f32[1536]{0:T(1024)}, u32[]{:S(2)}) copy-start(f32[1536]{0:T(1024)} %copy-done.153) | copy-start | bytes 18436
  300.4 29.7 %copy-start.126 = (f32[768]{0:T(1024)S(1)}, f32[768]{0:T(1024)}, u32[]{:S(2)}) copy-start(f32[768]{0:T(1024)} %copy-done.124) | copy-start | bytes 9220
  302.9 66.8 %reduce-scatter.25.cloned.1.call-start = ((), (), s32[]{:S(2)}) async-start(), calls=%async_computation.18 | async-start | bytes 1179648 | tf_op jit(solution)/shard_map/reduce_scatter | solution.py:222
  331.8 13.1 %copy-start.170 = (bf16[1,1536,768]{2,1,0:T(8,128)(2,1)S(1)}, bf16[1,1536,768]{2,1,0:T(8,128)(2,1)}, u32[]{:S(2)}) copy-start(bf16[1,1536,768]{2,1,0:T(8,128)(2,1)} %param.30) | copy-start | bytes 7077892
  331.9 13.1 %copy-start.175 = (f32[512,1536]{1,0:T(8,128)S(1)}, f32[512,1536]{1,0:T(8,128)}, u32[]{:S(2)}) copy-start(f32[512,1536]{1,0:T(8,128)} %get-tuple-element.307) | copy-start | bytes 9437188
  331.9 15.9 %copy-start.148 = (f32[256]{0:T(256)}, f32[256]{0:T(256)S(1)}, u32[]{:S(2)}) copy-start(f32[256]{0:T(256)S(1)} %broadcast_multiply_fusion.11) | copy-start | bytes 3076
  332.1 15.6 %copy-start.152 = (f32[256]{0:T(256)}, f32[256]{0:T(256)S(1)}, u32[]{:S(2)}) copy-start(f32[256]{0:T(256)S(1)} %add_rsqrt_fusion) | copy-start | bytes 3076
  351.2 68.1 %reduce-scatter.27.cloned.1.call-start = ((), (), s32[]{:S(2)}) async-start(), calls=%async_computation.19 | async-start | bytes 1179648 | tf_op jit(solution)/shard_map/reduce_scatter | solution.py:304
  369.7 15.7 %copy-start.33 = (bf16[1,384,768]{2,1,0:T(8,128)(2,1)S(1)}, bf16[1,384,768]{2,1,0:T(8,128)(2,1)}, u32[]{:S(2)}) copy-start(bf16[1,384,768]{2,1,0:T(8,128)(2,1)} %param.24) | copy-start | bytes 1769476
  372.3 14.0 %copy-start.113 = (bf16[512,384]{0,1:T(8,128)(2,1)S(1)}, bf16[512,384]{0,1:T(8,128)(2,1)}, u32[]{:S(2)}) copy-start(bf16[512,384]{0,1:T(8,128)(2,1)} %copy-done.112) | copy-start | bytes 1179652
  374.7 11.2 %copy-start.21 = (f32[1,256,768]{2,1,0:T(8,128)}, f32[1,256,768]{2,1,0:T(8,128)S(1)}, u32[]{:S(2)}) copy-start(f32[1,256,768]{2,1,0:T(8,128)S(1)} %get-tuple-element.256) | copy-start | bytes 2359300
  399.4 25.5 %copy-start.134 = (f32[256]{0:T(256)S(1)}, f32[256]{0:T(256)}, u32[]{:S(2)}) copy-start(f32[256]{0:T(256)} %copy-done.133) | copy-start | bytes 3076
  399.4 25.5 %copy-start.140 = (f32[256]{0:T(256)S(1)}, f32[256]{0:T(256)}, u32[]{:S(2)}) copy-start(f32[256]{0:T(256)} %copy-done.139) | copy-start | bytes 3076
  400.9 62.6 %reduce-scatter.29.cloned.1.call-start = ((), (), s32[]{:S(2)}) async-start(), calls=%async_computation.20 | async-start | bytes 1179648 | tf_op jit(solution)/shard_map/reduce_scatter | solution.py:222
  420.7 18.4 %copy-start.171 = (bf16[1,1536,768]{2,1,0:T(8,128)(2,1)S(1)}, bf16[1,1536,768]{2,1,0:T(8,128)(2,1)}, u32[]{:S(2)}) copy-start(bf16[1,1536,768]{2,1,0:T(8,128)(2,1)} %param.30) | copy-start | bytes 7077892
  420.7 18.4 %copy-start.174 = (f32[512,1536]{1,0:T(8,128)S(1)}, f32[512,1536]{1,0:T(8,128)}, u32[]{:S(2)}) copy-start(f32[512,1536]{1,0:T(8,128)} %get-tuple-element.303) | copy-start | bytes 9437188
  420.7 4.2 collective-permute-start.2
  445.4 66.9 %reduce-scatter.31.cloned.1.call-start = ((), (), s32[]{:S(2)}) async-start(), calls=%async_computation.21 | async-start | bytes 1179648 | tf_op jit(solution)/shard_map/reduce_scatter | solution.py:304
  446.3 38.2 %copy-start.115 = (f32[6,512]{1,0:T(8,128)}, f32[6,512]{1,0:T(8,128)S(1)}, u32[]{:S(2)}) copy-start(f32[6,512]{1,0:T(8,128)S(1)} %log_add_fusion.1) | copy-start | bytes 36868
  451.6 11.9 %copy-start.138 = (f32[256]{0:T(256)S(1)}, f32[256]{0:T(256)}, u32[]{:S(2)}) copy-start(f32[256]{0:T(256)} %copy-done.137) | copy-start | bytes 3076
  451.6 11.9 %copy-start.147 = (f32[256]{0:T(256)S(1)}, f32[256]{0:T(256)}, u32[]{:S(2)}) copy-start(f32[256]{0:T(256)} %copy-done.146) | copy-start | bytes 3076
  463.5 15.7 %copy-start.34 = (bf16[1,384,768]{2,1,0:T(8,128)(2,1)S(1)}, bf16[1,384,768]{2,1,0:T(8,128)(2,1)}, u32[]{:S(2)}) copy-start(bf16[1,384,768]{2,1,0:T(8,128)(2,1)} %param.24) | copy-start | bytes 1769476
  466.1 14.0 %copy-start.111 = (bf16[512,384]{0,1:T(8,128)(2,1)S(1)}, bf16[512,384]{0,1:T(8,128)(2,1)}, u32[]{:S(2)}) copy-start(bf16[512,384]{0,1:T(8,128)(2,1)} %copy-done.110) | copy-start | bytes 1179652
  493.8 65.5 %reduce-scatter.33.cloned.1.call-start = ((), (), s32[]{:S(2)}) async-start(), calls=%async_computation.22 | async-start | bytes 1179648 | tf_op jit(solution)/shard_map/reduce_scatter | solution.py:222
  515.0 7.0 collective-permute-start.3
  522.0 13.7 %copy-start.172 = (bf16[1,1536,768]{2,1,0:T(8,128)(2,1)S(1)}, bf16[1,1536,768]{2,1,0:T(8,128)(2,1)}, u32[]{:S(2)}) copy-start(bf16[1,1536,768]{2,1,0:T(8,128)(2,1)} %param.30) | copy-start | bytes 7077892
  522.0 13.7 %copy-start.173 = (f32[512,1536]{1,0:T(8,128)S(1)}, f32[512,1536]{1,0:T(8,128)}, u32[]{:S(2)}) copy-start(f32[512,1536]{1,0:T(8,128)} %get-tuple-element.299) | copy-start | bytes 9437188
  542.1 160.9 %reduce-scatter.35.cloned.1.call-start = ((), (), s32[]{:S(2)}) async-start(), calls=%async_computation.23 | async-start | bytes 1179648 | tf_op jit(solution)/shard_map/reduce_scatter | solution.py:304
  559.4 15.9 %copy-start.35 = (bf16[1,384,768]{2,1,0:T(8,128)(2,1)S(1)}, bf16[1,384,768]{2,1,0:T(8,128)(2,1)}, u32[]{:S(2)}) copy-start(bf16[1,384,768]{2,1,0:T(8,128)(2,1)} %param.24) | copy-start | bytes 1769476
  562.0 14.2 %copy-start.114 = (f32[6,512]{1,0:T(8,128)S(1)}, f32[6,512]{1,0:T(8,128)}, u32[]{:S(2)}) copy-start(f32[6,512]{1,0:T(8,128)} %log_add_fusion.2) | copy-start | bytes 36868
  564.4 11.5 %copy-start.22 = (f32[1,256,768]{2,1,0:T(8,128)}, f32[1,256,768]{2,1,0:T(8,128)S(1)}, u32[]{:S(2)}) copy-start(f32[1,256,768]{2,1,0:T(8,128)S(1)} %get-tuple-element.260) | copy-start | bytes 2359300
  593.5 467.2 %all-reduce.5.cloned.1.call-start = ((), (), s32[]{:S(2)}) async-start(), calls=%async_computation.24 | async-start | bytes 28311552 | tf_op jit(solution)/shard_map/psum | solution.py:442
  608.6 94.3 %copy-start.141 = (f32[256]{0:T(256)S(1)}, f32[256]{0:T(256)}, u32[]{:S(2)}) copy-start(f32[256]{0:T(256)} %copy-done.139) | copy-start | bytes 3076
  608.6 95.8 %copy-start.104 = (bf16[1,256,768]{2,1,0:T(8,128)(2,1)S(1)}, bf16[1,256,768]{2,1,0:T(8,128)(2,1)}, u32[]{:S(2)}) copy-start(bf16[1,256,768]{2,1,0:T(8,128)(2,1)} %get-tuple-element.292) | copy-start | bytes 1179652
  (137 other events, 502.1 us)
Sparse Core Ops, SparseCore 0:
  33.4 28.0 reduce-scatter.12
  87.6 26.9 reduce-scatter.14
  141.2 26.3 reduce-scatter.16
  194.2 26.9 reduce-scatter.18
  250.3 26.3 reduce-scatter.20
  303.1 26.9 reduce-scatter.22
  351.4 18.3 reduce-scatter.24
  401.0 18.3 reduce-scatter.26
  445.5 17.9 reduce-scatter.28
  494.0 18.3 reduce-scatter.30
  542.2 17.1 reduce-scatter.32
  593.6 18.3 reduce-scatter.34
  618.5 442.2 all-reduce.4
where the time goes:
time: 1090 us; the launch traced here: 1080 us
  waiting for transfers between devices  575 us (53%)
  blocking collectives  212 us (19%)
  matrix products  169 us (16%)
  other arithmetic  61.1 us (6%)
  local copies, waits for them, and re-layouts  35.1 us (3%)
  between operations  16.4 us (2%)
    psum x1, waiting for transfers between devices, shards(): lax.psum((attention_acc[0], attention_acc[1], attention_acc[2], attention...  355 us
    reduce_scatter x3, waiting for transfers between devices, layer_forward(): lax.psum_scatter(partial_ffn.reshape(slot_count, slot_size, model_width),...  81.1 us
    reduce_scatter x3, waiting for transfers between devices, layer_forward(): lax.psum_scatter(partial_attention.reshape(slot_count, slot_size, model_w...  80.9 us
    psum x1, blocking collectives, shards(): lax.psum((small_acc[0], small_acc[1], small_acc[2], small_acc[3], small_a...  65.7 us
    all_gather x3, blocking collectives, layer_forward(): full_rows = lax.all_gather(half_rows, 'tensor', axis=1, tiled=True)  33.5 us
    all_gather x3, blocking collectives, backward_ffn(): lax.all_gather(grad_residue_two.astype(jnp.bfloat16), 'tensor', axis=1, t...  33.1 us
    all_gather x3, blocking collectives, backward_attention(): lax.all_gather(grad_residue_one.astype(jnp.bfloat16), 'tensor', axis=1, t...  32.2 us
    all_gather x3, blocking collectives, layer_forward(): lax.all_gather(normed.astype(jnp.bfloat16), 'tensor', axis=1, tiled=True)  32 us
  transfers between devices with their start and end apart: 17, of which 15 were waited for; matrix products, arithmetic and copies ran while one was open for 7% of the time, Pallas kernels for 0%

commit v1 on v0

v1 whole, which is shorter than its diff:
```python
import functools
import math

import jax
import jax.numpy as jnp
from jax import lax
from jax.experimental import pallas as pl
from jax.experimental.pallas import tpu as pltpu
from jax.sharding import PartitionSpec as P

HD = 64
epsilon = 1e-06
root_half = 0.7071067811865476
inverse_root = 0.3989422804014327
BF = jnp.bfloat16
F32 = jnp.float32
RB = 128
VMEM_BYTES = 56 * 1024 * 1024

V_BQV, V_BO, V_G1, V_B1, V_BI, V_BU, V_G2, V_B2 = 0, 1, 2, 3, 4, 6, 7, 8
V_ROWS = 16
SMALL_ROWS = 32


def dot(a, b):
    return lax.dot_general(a, b, (((1,), (0,)), ((), ())), preferred_element_type=F32)


def dot_nt(a, b):
    return lax.dot_general(a, b, (((1,), (1,)), ((), ())), preferred_element_type=F32)


def dot_tn(a, b):
    return lax.dot_general(a, b, (((0,), (0,)), ((), ())), preferred_element_type=F32)


def start_fetch(use_own, own, other, held, sems):
    @pl.when(use_own)
    def _():
        for i in range(len(own)):
            pltpu.make_async_copy(own[i], held[i], sems.at[i]).start()

    @pl.when(jnp.logical_not(use_own))
    def _():
        for i in range(len(own)):
            pltpu.make_async_copy(other[i], held[i], sems.at[i]).start()


def wait_fetch(i, own, held, sems):
    pltpu.make_async_copy(own[i], held[i], sems.at[i]).wait()


def row_blocks(total, body):
    def step(i, carry):
        body(pl.ds(pl.multiple_of(i * RB, RB), RB))
        return carry

    lax.fori_loop(0, total // RB, step, 0)


def norm_rows(residue):
    center = residue - jnp.mean(residue, axis=-1, keepdims=True)
    inverse = lax.rsqrt(jnp.mean(center * center, axis=-1, keepdims=True) + epsilon)
    return center * inverse, inverse


def norm_back_rows(upstream, normal, inverse, gain):
    scaled = upstream * gain
    centred = scaled - jnp.mean(scaled, axis=-1, keepdims=True)
    return (centred - normal * jnp.mean(scaled * normal, axis=-1, keepdims=True)) * inverse


def column_sum(rows):
    return jnp.sum(rows, axis=0, keepdims=True)


def segment_bias(flags, bias):
    size = bias.shape[0]
    ends = [flags[2]]
    for i in range(3, 5):
        ends.append(ends[-1] + flags[i])
    row = lax.broadcasted_iota(jnp.int32, (1, size), 1)
    row_seg = sum((row >= e).astype(jnp.int32) for e in ends)

    def body(rows):
        col = lax.broadcasted_iota(jnp.int32, (RB, 1), 0) + rows.start
        col_seg = sum((col >= e).astype(jnp.int32) for e in ends)
        bias[rows, :] = jnp.where(col_seg == row_seg, 0.0, -1e30).astype(F32)

    row_blocks(size, body)


def attention_forward(flags, x, vec, weights, wait, outs, scratch):
    wq, wk, wv, wo = weights
    q_out, k_out, v_out, e_out, r_out, o_out, ot_out, p_out = outs
    qt_s, kh_s, vt_s, bias = scratch
    size = x.shape[0]
    width = wq.shape[1]
    heads = width // HD
    segment_bias(flags, bias)
    wait(0)
    wait(1)
    wait(2)
    for i in range(size // 256):
        rows = pl.ds(i * 256, 256)
        xb = x[rows, :]
        q = (dot(xb, wq[...]) + vec[V_BQV : V_BQV + 1, :width]).astype(BF).astype(F32) * (
            1.0 / math.sqrt(HD)
        )
        q_out[rows, :] = q.astype(BF)
        qt_s[:, rows] = q.T.astype(BF)
        k = dot(xb, wk[...]).astype(BF)
        k_out[rows, :] = k
        for h in range(heads):
            kh_s[h, rows, :] = k[:, h * HD : (h + 1) * HD]
        v = dot(xb, wv[...]) + vec[V_BQV : V_BQV + 1, width : 2 * width]
        v_out[rows, :] = v.astype(BF)
        vt_s[:, rows] = v.T.astype(BF)
    for h in range(heads):
        hs = slice(h * HD, (h + 1) * HD)
        for j in range(size // 256):
            cols = pl.ds(j * 256, 256)
            scores = dot(kh_s[h], qt_s[hs, cols]) + bias[:, cols]
            highest = jnp.max(scores, axis=0, keepdims=True)
            raised = jnp.exp(scores - highest)
            inverse = 1.0 / jnp.sum(raised, axis=0, keepdims=True)
            raised = raised.astype(BF)
            e_out[h, :, cols] = raised
            r_out[h : h + 1, cols] = inverse
            ot_out[hs, cols] = dot(vt_s[hs, :], raised) * inverse
    wait(3)
    for i in range(size // 256):
        rows = pl.ds(i * 256, 256)
        context = ot_out[:, rows].T.astype(BF)
        o_out[rows, :] = context
        p_out[rows, :] = dot(context, wo[...]).astype(BF)


def attention_first_kernel(
    flags, own, far, peer_a, peer_b, vec,
    wq, wk, wv, wo, wq2, wk2, wv2, wo2,
    x_out, q_out, k_out, v_out, e_out, r_out, o_out, ot_out, p_out,
    wq_s, wk_s, wv_s, wo_s, qt_s, kh_s, vt_s, bias, sems,
):
    first = flags[0] == 0
    held = (wq_s, wk_s, wv_s, wo_s)
    source = (wq, wk, wv, wo)
    start_fetch(first, source, (wq2, wk2, wv2, wo2), held, sems)
    half = own.shape[0]
    mine = pl.multiple_of(flags[1] * half, half)
    theirs = pl.multiple_of((1 - flags[1]) * half, half)
    x_out[pl.ds(mine, half), :] = jnp.where(first, own[...], far[...])
    x_out[pl.ds(theirs, half), :] = jnp.where(first, peer_a[...], peer_b[...])
    attention_forward(
        flags, x_out, vec, held, lambda i: wait_fetch(i, source, held, sems),
        (q_out, k_out, v_out, e_out, r_out, o_out, ot_out, p_out), (qt_s, kh_s, vt_s, bias),
    )


def attention_next_kernel(
    flags, normal_one, part_a, part_b, vec_prev, vec,
    wq, wk, wv, wo, wq2, wk2, wv2, wo2,
    n2_out, i2_out, x_out, q_out, k_out, v_out, e_out, r_out, o_out, ot_out, p_out,
    wq_s, wk_s, wv_s, wo_s, qt_s, kh_s, vt_s, bias, sems,
):
    held = (wq_s, wk_s, wv_s, wo_s)
    source = (wq, wk, wv, wo)
    start_fetch(flags[0] == 1, source, (wq2, wk2, wv2, wo2), held, sems)

    def body(rows):
        normal, inverse, output = second_norm(normal_one, part_a, part_b, vec_prev, rows)
        n2_out[rows, :] = normal
        i2_out[rows, :] = inverse
        x_out[rows, :] = output.astype(BF)

    row_blocks(x_out.shape[0], body)
    attention_forward(
        flags, x_out, vec, held, lambda i: wait_fetch(i, source, held, sems),
        (q_out, k_out, v_out, e_out, r_out, o_out, ot_out, p_out), (qt_s, kh_s, vt_s, bias),
    )


def second_norm(normal_one, part_a, part_b, vec, rows):
    normed = normal_one[rows, :] * vec[V_G1 : V_G1 + 1, :] + vec[V_B1 : V_B1 + 1, :]
    total = part_a[rows, :].astype(F32) + part_b[rows, :].astype(F32)
    normal, inverse = norm_rows(total + vec[V_BU : V_BU + 1, :] + normed)
    return normal, inverse, normal * vec[V_G2 : V_G2 + 1, :] + vec[V_B2 : V_B2 + 1, :]


def ffn_forward_kernel(
    layer, flags, x, part_a, part_b, vec, wi, wu, wi2, wu2,
    n1_out, i1_out, n1b_out, a_out, d_out, p_out,
    wi_s, wu_s, sems,
):
    held = (wi_s, wu_s)
    source = (wi, wu)
    start_fetch(flags[0] == layer, source, (wi2, wu2), held, sems)
    size = x.shape[0]
    width = wi_s.shape[1]
    model = wi_s.shape[0]

    def first(rows):
        total = part_a[rows, :].astype(F32) + part_b[rows, :].astype(F32)
        normal, inverse = norm_rows(total + vec[V_BO : V_BO + 1, :] + x[rows, :].astype(F32))
        n1_out[rows, :] = normal
        i1_out[rows, :] = inverse
        n1b_out[rows, :] = (normal * vec[V_G1 : V_G1 + 1, :] + vec[V_B1 : V_B1 + 1, :]).astype(BF)

    row_blocks(size, first)
    wait_fetch(0, source, held, sems)
    block = 256

    def inner(rows):
        rows_in = n1b_out[rows, :]
        for j in range(width // block):
            cols = slice(j * block, (j + 1) * block)
            at = j * block
            bias = vec[V_BI + at // model : V_BI + at // model + 1, at % model : at % model + block]
            hidden = dot(rows_in, wi_s[:, cols]) + bias
            spread = 0.5 + 0.5 * lax.erf(hidden * root_half)
            a_out[rows, cols] = (hidden * spread).astype(BF)
            d_out[rows, cols] = (
                spread + hidden * jnp.exp(-0.5 * hidden * hidden) * inverse_root
            ).astype(BF)

    row_blocks(size, inner)
    wait_fetch(1, source, held, sems)
    for i in range(size // 256):
        rows = pl.ds(i * 256, 256)
        p_out[rows, :] = dot(a_out[rows, :], wu_s[...]).astype(BF)


def ffn_backward(g2, d, w, outs, wait, small):
    wi_s, wu_s = w
    gh_out, p_out = outs
    size = g2.shape[0]
    model, width = wi_s.shape
    wait(1)
    sums = [jnp.zeros((1, model), F32)] * (width // model)
    for i in range(size // 256):
        rows = pl.ds(i * 256, 256)
        gb = g2[rows, :]
        for j in range(width // 384):
            cols = slice(j * 384, (j + 1) * 384)
            gh_out[rows, cols] = (dot_nt(gb, wu_s[cols, :]) * d[rows, cols].astype(F32)).astype(BF)
    wait(0)
    for i in range(size // 256):
        rows = pl.ds(i * 256, 256)
        gh = gh_out[rows, :]
        for j in range(width // model):
            part = gh[:, j * model : (j + 1) * model].astype(F32)
            sums[j] = sums[j] + column_sum(part)
        p_out[rows, :] = dot_nt(gh, wi_s[...]).astype(BF)
    for j in range(width // model):
        small[3 + j : 4 + j, :] = sums[j]


def ffn_back_last_kernel(
    flags, normal_one, part_a, part_b, vec, own, far, peer_a, peer_b, d, wi, wu, wi2, wu2,
    y_out, g_out, gb_out, gh_out, p_out, small,
    gy_s, wi_s, wu_s, sems,
):
    held = (wi_s, wu_s)
    source = (wi, wu)
    second = flags[0] == 1
    start_fetch(second, source, (wi2, wu2), held, sems)
    half = own.shape[0]
    mine = pl.multiple_of(flags[1] * half, half)
    theirs = pl.multiple_of((1 - flags[1]) * half, half)
    gy_s[pl.ds(mine, half), :] = jnp.where(second, own[...], far[...])
    gy_s[pl.ds(theirs, half), :] = jnp.where(second, peer_a[...], peer_b[...])
    small[...] = jnp.zeros_like(small)

    def body(rows):
        normal, inverse, output = second_norm(normal_one, part_a, part_b, vec, rows)
        y_out[rows, :] = output.astype(BF)
        ffn_back_rows(gy_s[rows, :].astype(F32), normal, inverse, vec, rows, g_out, gb_out, small)

    row_blocks(y_out.shape[0], body)
    ffn_backward(gb_out, d, held, (gh_out, p_out), lambda i: wait_fetch(i, source, held, sems), small)


def ffn_back_rows(upstream, normal, inverse, vec, rows, g_out, gb_out, small):
    grad = norm_back_rows(upstream, normal, inverse, vec[V_G2 : V_G2 + 1, :])
    g_out[rows, :] = grad
    gb_out[rows, :] = grad.astype(BF)
    small[0:1, :] += column_sum(grad)
    small[1:2, :] += column_sum(upstream * normal)
    small[2:3, :] += column_sum(upstream)


def ffn_back_next_kernel(
    flags, g1, part_a, part_b, normal_two, inverse_two, vec, d, wi, wu, wi2, wu2,
    g_out, gb_out, gh_out, p_out, small,
    wi_s, wu_s, sems,
):
    held = (wi_s, wu_s)
    source = (wi, wu)
    start_fetch(flags[0] == 0, source, (wi2, wu2), held, sems)
    small[...] = jnp.zeros_like(small)

    def body(rows):
        total = part_a[rows, :].astype(F32) + part_b[rows, :].astype(F32)
        upstream = (g1[rows, :] + total).astype(BF).astype(F32)
        ffn_back_rows(
            upstream, normal_two[rows, :], inverse_two[rows, :], vec, rows, g_out, gb_out, small
        )

    row_blocks(g1.shape[0], body)
    ffn_backward(gb_out, d, held, (gh_out, p_out), lambda i: wait_fetch(i, source, held, sems), small)


def attention_back_kernel(
    layer, flags, g2, part_a, part_b, normal_one, inverse_one, vec, q, k, v, e, r, ot_f,
    wq, wk, wv, wo, wq2, wk2, wv2, wo2,
    g_out, gb_out, gqkv_out, p_out, small,
    wq_s, wk_s, wv_s, wo_s, got_s, go_s, kt_s, vh_s, qh_s, gqt_s, delta_s, sems,
):
    held = (wq_s, wk_s, wv_s, wo_s)
    source = (wq, wk, wv, wo)
    start_fetch(flags[0] == layer, source, (wq2, wk2, wv2, wo2), held, sems)
    size, model = g2.shape
    width = q.shape[1]
    heads = width // HD
    small[...] = jnp.zeros_like(small)

    def body(rows):
        total = part_a[rows, :].astype(F32) + part_b[rows, :].astype(F32)
        upstream = g2[rows, :] + total
        normal = normal_one[rows, :]
        grad = norm_back_rows(upstream, normal, inverse_one[rows, :], vec[V_G1 : V_G1 + 1, :])
        g_out[rows, :] = grad
        gb_out[rows, :] = grad.astype(BF)
        small[0:1, :] += column_sum(grad)
        small[1:2, :] += column_sum(upstream * normal)
        small[2:3, :] += column_sum(upstream)

    row_blocks(size, body)
    for i in range(size // 256):
        rows = pl.ds(i * 256, 256)
        kt_s[:, rows] = k[rows, :].astype(F32).T.astype(BF)
        for h in range(heads):
            hs = slice(h * HD, (h + 1) * HD)
            vh_s[h, rows, :] = v[rows, hs]
            qh_s[h, rows, :] = q[rows, hs]
    wait_fetch(3, source, held, sems)
    for i in range(size // 256):
        rows = pl.ds(i * 256, 256)
        got = dot_nt(gb_out[rows, :], wo_s[...]).T
        for h in range(heads):
            hs = slice(h * HD, (h + 1) * HD)
            scaled = (got[hs, :] * r[h : h + 1, rows]).astype(BF)
            got_s[hs, rows] = scaled
            scaled = scaled.astype(F32)
            delta_s[h : h + 1, rows] = column_sum(scaled * ot_f[hs, rows])
            go_s[h, rows, :] = scaled.T.astype(BF)
    for h in range(heads):
        hs = slice(h * HD, (h + 1) * HD)
        grad_v = jnp.zeros((size, HD), F32)
        grad_k = jnp.zeros((size, HD), F32)
        for j in range(size // 256):
            cols = pl.ds(j * 256, 256)
            raised = e[h, :, cols]
            grad_p = dot(vh_s[h], got_s[hs, cols]) - delta_s[h : h + 1, cols]
            grad_s = (raised.astype(F32) * grad_p).astype(BF)
            grad_v = grad_v + dot(raised, go_s[h, cols, :])
            grad_k = grad_k + dot(grad_s, qh_s[h, cols, :])
            gqt_s[hs, cols] = dot(kt_s[hs, :], grad_s) * (1.0 / math.sqrt(HD))
        gqkv_out[:, width + h * HD : width + (h + 1) * HD] = grad_k.astype(BF)
        gqkv_out[:, 2 * width + h * HD : 2 * width + (h + 1) * HD] = grad_v.astype(BF)
    wait_fetch(0, source, held, sems)
    wait_fetch(1, source, held, sems)
    wait_fetch(2, source, held, sems)
    sum_q = jnp.zeros((1, width), F32)
    sum_v = jnp.zeros((1, width), F32)
    for i in range(size // 256):
        rows = pl.ds(i * 256, 256)
        gq = gqt_s[:, rows].T.astype(BF)
        gqkv_out[rows, :width] = gq
        gk = gqkv_out[rows, width : 2 * width]
        gv = gqkv_out[rows, 2 * width :]
        sum_q = sum_q + column_sum(gq.astype(F32))
        sum_v = sum_v + column_sum(gv.astype(F32))
        p_out[rows, :] = (
            dot_nt(gq, wq_s[...]) + dot_nt(gk, wk_s[...]) + dot_nt(gv, wv_s[...])
        ).astype(BF)
    small[3:4, :width] = sum_q
    small[3:4, width:] = sum_v


def call(kernel, operands, spaces, outs, scratch, flops):
    specs = {
        "s": pl.BlockSpec(memory_space=pltpu.SMEM),
        "v": pl.BlockSpec(memory_space=pltpu.VMEM),
        "a": pl.BlockSpec(memory_space=pl.ANY),
    }
    return pl.pallas_call(
        kernel,
        out_shape=[jax.ShapeDtypeStruct(s, t) for s, t in outs],
        in_specs=[specs[c] for c in spaces],
        out_specs=[specs["v"]] * len(outs),
        scratch_shapes=scratch,
        compiler_params=pltpu.CompilerParams(vmem_limit_bytes=VMEM_BYTES),
        cost_estimate=pl.CostEstimate(flops=flops, bytes_accessed=8 << 20, transcendentals=0),
    )(*operands)


def attention_call(flags, lead, lead_spaces, weights, size, model, width, kernel, extra_outs):
    heads = width // HD
    outs = extra_outs + [
        ((size, model), BF),
        ((size, width), BF),
        ((size, width), BF),
        ((size, width), BF),
        ((heads, size, size), BF),
        ((heads, size), F32),
        ((size, width), BF),
        ((width, size), F32),
        ((size, model), BF),
    ]
    scratch = [pltpu.VMEM((model, width), BF)] * 3 + [
        pltpu.VMEM((width, model), BF),
        pltpu.VMEM((width, size), BF),
        pltpu.VMEM((heads, size, HD), BF),
        pltpu.VMEM((width, size), BF),
        pltpu.VMEM((size, size), F32),
        pltpu.SemaphoreType.DMA((4,)),
    ]
    return call(
        kernel, (flags,) + lead + weights, "s" + lead_spaces + "a" * 8, outs, scratch,
        2 * size * width * model * 4 + 4 * heads * size * size * HD,
    )


def swap(block, axis):
    return lax.ppermute(block, axis, [(0, 1), (1, 0)])


def across(block, routes):
    return lax.ppermute(
        block, ("section", "tensor"), [(a[0] * 2 + a[1], b[0] * 2 + b[1]) for a, b in routes]
    )


def reduce_rows(block, x_first):
    count = lax.axis_size("batch")
    place = lax.axis_index("batch")

    def send(rows, pairs):
        return lax.ppermute(rows, "batch", pairs)

    if count != 8:
        if count & (count - 1):
            return lax.psum(block, "batch")
        step = 1
        while step < count:
            block = block + send(block, [(i, i ^ step) for i in range(count)])
            step *= 2
        return block
    half = block.shape[0] // 2
    side = place % 2
    line = place // 2
    inward = [(0, 2), (1, 3), (6, 4), (7, 5)]
    middle = [(2, 4), (3, 5), (4, 2), (5, 3)]
    outward = [(b, a) for a, b in inward]
    edge = (line == 0) | (line == 3)

    def part(which):
        return lax.dynamic_slice_in_dim(block, which * half, half, 0)

    def join(which, mine, theirs):
        low = jnp.where(which == 0, mine, theirs)
        high = jnp.where(which == 0, theirs, mine)
        return jnp.concatenate([low, high], axis=0)

    if x_first:
        pairs = [(i, i ^ 1) for i in range(8)]
        mine = part(side) + send(part(1 - side), pairs)
        mine = mine + send(mine, inward)
        mine = mine + send(mine, middle)
        mine = jnp.where(edge, send(mine, outward), mine)
        return join(side, mine, send(mine, pairs))
    block = block + send(block, inward)
    which = (line >= 2).astype(jnp.int32)
    mine = part(which) + send(part(1 - which), middle)
    mine = mine + send(mine, [(i, i ^ 1) for i in range(2, 6)])
    block = join(which, mine, send(mine, middle))
    return jnp.where(edge, send(block, outward), block)


def pad_rows(rows, count):
    return jnp.concatenate([rows, jnp.zeros((count - rows.shape[0], rows.shape[1]), rows.dtype)], 0)


def shards(
    section_ends, lengths, w_query, b_query, w_key, w_value, b_value, w_out, b_out,
    norm1_gain, norm1_bias, w_inner, b_inner, w_outer, b_outer, norm2_gain, norm2_bias,
):
    section = lax.axis_index("section")
    tensor = lax.axis_index("tensor")
    first = section == 0
    held = section_ends[0]
    half, model = held.shape[1], held.shape[2]
    size = 2 * half
    width = w_query.shape[2]
    inner = w_inner.shape[2]
    heads = width // HD
    flags = jnp.concatenate(
        [
            jnp.stack([section, tensor]).astype(jnp.int32),
            lax.dynamic_slice_in_dim(lengths, section, 1, 0)[0],
        ]
    )

    x_peer_a = across(held[0], [((0, 0), (0, 1)), ((0, 1), (0, 0))])
    x_peer_b = across(held[1], [((0, 0), (1, 1)), ((0, 1), (1, 0))])
    x_far = across(held[1], [((0, 0), (1, 0)), ((0, 1), (1, 1))])

    attention_own = (w_query[0], w_key[0], w_value[0], w_out[0])
    ffn_own = (w_inner[0], w_outer[0])
    vec_own = pad_rows(
        jnp.concatenate(
            [
                jnp.concatenate([b_query, b_value], axis=1),
                b_out, norm1_gain, norm1_bias, b_inner.reshape(-1, model), b_outer,
                norm2_gain, norm2_bias,
            ],
            axis=0,
        ),
        V_ROWS,
    )
    vec_far = swap(vec_own, "section")
    attention_far = tuple(swap(w, "section") for w in attention_own)
    ffn_far = tuple(swap(w, "section") for w in ffn_own)
    attention_w = attention_own + attention_far
    ffn_w = ffn_own + ffn_far
    vec_one = jnp.where(first, vec_own, vec_far)
    vec_two = jnp.where(first, vec_far, vec_own)

    gy_peer_a = across(held[1], [((1, 0), (1, 1)), ((1, 1), (1, 0))])
    gy_peer_b = across(held[0], [((1, 0), (0, 1)), ((1, 1), (0, 0))])
    gy_far = across(held[0], [((1, 0), (0, 0)), ((1, 1), (0, 1))])

    def ffn_forward(layer, x, part, vec):
        return call(
            functools.partial(ffn_forward_kernel, layer),
            (flags, x, part, swap(part, "tensor"), vec) + ffn_w,
            "svvvvaaaa",
            [
                ((size, model), F32), ((size, 1), F32), ((size, model), BF),
                ((size, inner), BF), ((size, inner), BF), ((size, model), BF),
            ],
            [
                pltpu.VMEM((model, inner), BF), pltpu.VMEM((inner, model), BF),
                pltpu.SemaphoreType.DMA((2,)),
            ],
            4 * size * model * inner,
        )

    x_one, *heads_one, part = attention_call(
        flags, (held[0], x_far, x_peer_a, x_peer_b, vec_one), "vvvvv", attention_w,
        size, model, width, attention_first_kernel, [],
    )
    n1_one, i1_one, n1b_one, a_one, d_one, part = ffn_forward(0, x_one, part, vec_one)
    n2_one, i2_one, x_two, *heads_two, part = attention_call(
        flags, (n1_one, part, swap(part, "tensor"), vec_one, vec_two), "vvvvv", attention_w,
        size, model, width, attention_next_kernel, [((size, model), F32), ((size, 1), F32)],
    )
    n1_two, i1_two, n1b_two, a_two, d_two, part = ffn_forward(1, x_two, part, vec_two)

    ffn_outs = [
        ((size, model), F32), ((size, model), BF), ((size, inner), BF), ((size, model), BF),
        ((8, model), F32),
    ]
    ffn_scratch = [
        pltpu.VMEM((model, inner), BF), pltpu.VMEM((inner, model), BF),
        pltpu.SemaphoreType.DMA((2,)),
    ]

    def reduce_pair(first_left, first_right, second_left, second_right, small, x_first):
        def product(left, right):
            return lax.dot_general(
                left, right, (((0,), (0,)), ((), ())), preferred_element_type=F32
            ).astype(BF)

        def both(pairs):
            return jnp.concatenate([product(*p) for p in pairs] + [small], axis=0)

        one, two = zip(first_left, first_right), zip(second_left, second_right)
        one, two = list(one), list(two)
        sent = [
            (jnp.where(first, b[0], a[0]), jnp.where(first, b[1], a[1])) for a, b in zip(one, two)
        ]
        kept = [
            (jnp.where(first, a[0], b[0]), jnp.where(first, a[1], b[1])) for a, b in zip(one, two)
        ]
        got = swap(both(sent), "section")
        return reduce_rows(both(kept) + got, x_first)

    def ffn_reduce(a, gb, gh, n1b, small, x_first):
        return reduce_pair(
            (a,), (gb,), (gh,), (n1b,), pad_rows(small.astype(BF), SMALL_ROWS), x_first
        )

    def attention_back(layer, g2, part, n1, i1, vec, saved):
        q, k, v, e, r, o, ot_f = saved
        return call(
            functools.partial(attention_back_kernel, layer),
            (flags, g2, part, swap(part, "tensor"), n1, i1, vec, q, k, v, e, r, ot_f) + attention_w,
            "s" + "v" * 12 + "a" * 8,
            [
                ((size, model), F32), ((size, model), BF), ((size, 3 * width), BF),
                ((size, model), BF), ((8, model), F32),
            ],
            [pltpu.VMEM((model, width), BF)] * 3
            + [
                pltpu.VMEM((width, model), BF),
                pltpu.VMEM((width, size), BF),
                pltpu.VMEM((heads, size, HD), BF),
                pltpu.VMEM((width, size), BF),
                pltpu.VMEM((heads, size, HD), BF),
                pltpu.VMEM((heads, size, HD), BF),
                pltpu.VMEM((width, size), F32),
                pltpu.VMEM((8, size), F32),
                pltpu.SemaphoreType.DMA((4,)),
            ],
            2 * size * width * model * 4 + 8 * heads * size * size * HD,
        )

    def attention_reduce(gqkv, x, o, gb, small, x_first):
        gq, gk, gv = (gqkv[:, i * width : (i + 1) * width] for i in range(3))
        return reduce_pair(
            (gq, gk), (x, x), (gv, o), (x, gb), pad_rows(small.astype(BF), SMALL_ROWS), x_first
        )

    y_two, g2_two, g2b_two, gh_two, part, small_f2 = call(
        ffn_back_last_kernel,
        (flags, n1_two, part, swap(part, "tensor"), vec_two, held[1], gy_far, gy_peer_a, gy_peer_b,
         d_two) + ffn_w,
        "s" + "v" * 9 + "a" * 4,
        [((size, model), BF)] + ffn_outs,
        [pltpu.VMEM((size, model), BF)] + ffn_scratch,
        4 * size * model * inner,
    )
    sum_f2 = ffn_reduce(a_two, g2b_two, gh_two, n1b_two, small_f2, True)
    g1_two, g1b_two, gqkv_two, part, small_a2 = attention_back(
        1, g2_two, part, n1_two, i1_two, vec_two, heads_two
    )
    sum_a2 = attention_reduce(gqkv_two, x_two, heads_two[5], g1b_two, small_a2, False)

    g2_one, g2b_one, gh_one, part, small_f1 = call(
        ffn_back_next_kernel,
        (flags, g1_two, part, swap(part, "tensor"), n2_one, i2_one, vec_one, d_one) + ffn_w,
        "s" + "v" * 7 + "a" * 4,
        ffn_outs,
        ffn_scratch,
        4 * size * model * inner,
    )
    sum_f1 = ffn_reduce(a_one, g2b_one, gh_one, n1b_one, small_f1, False)
    g1_one, g1b_one, gqkv_one, part, small_a1 = attention_back(
        0, g2_one, part, n1_one, i1_one, vec_one, heads_one
    )
    sum_a1 = attention_reduce(gqkv_one, x_one, heads_one[5], g1b_one, small_a1, True)

    part_mine = lax.dynamic_slice_in_dim(part, tensor * half, half, 0)
    part_theirs = lax.dynamic_slice_in_dim(part, (1 - tensor) * half, half, 0)
    total = part_mine.astype(F32) + swap(part_theirs, "tensor").astype(F32)
    gx = (lax.dynamic_slice_in_dim(g1_one, tensor * half, half, 0) + total).astype(BF)
    y_mine = lax.dynamic_slice_in_dim(y_two, tensor * half, half, 0)
    y_far = lax.ppermute(y_mine, "section", [(0, 1)])
    gx_far = lax.ppermute(gx, "section", [(1, 0)])
    section_results = jnp.stack(
        [jnp.where(first, gx, y_far), jnp.where(first, gx_far, y_mine)], axis=0
    )[None]

    def exchange(sum_one, sum_two):
        far_two = lax.ppermute(sum_two, "section", [(0, 1)])
        far_one = lax.ppermute(sum_one, "section", [(1, 0)])
        return (
            jnp.where(first, sum_one, far_two).astype(F32),
            jnp.where(first, far_one, sum_two).astype(F32),
        )

    ffn_first, ffn_second = exchange(sum_f1, sum_f2)
    att_first, att_second = exchange(sum_a1, sum_a2)
    small_f = ffn_first[inner:]
    small_a = att_first[2 * width :]
    return (
        section_results,
        att_first[:width].T[None],
        small_a[3:4, :width],
        att_first[width : 2 * width].T[None],
        att_second[:width].T[None],
        small_a[3:4, width:],
        att_second[width : 2 * width][None],
        small_a[0:1],
        small_a[1:2],
        small_a[2:3],
        ffn_second[:inner].T[None],
        small_f[3 : 3 + inner // model].reshape(1, inner),
        ffn_first[:inner][None],
        small_f[0:1],
        small_f[1:2],
        small_f[2:3],
    )


def solution(mesh):
    in_specs = (
        P("section", "batch", "tensor", None),
        P("batch", None),
        P("section", None, "tensor"),
        P("section", "tensor"),
        P("section", None, "tensor"),
        P("section", None, "tensor"),
        P("section", "tensor"),
        P("section", "tensor", None),
        P("section", None),
        P("section", None),
        P("section", None),
        P("section", None, "tensor"),
        P("section", "tensor"),
        P("section", "tensor", None),
        P("section", None),
        P("section", None),
        P("section", None),
    )
    out_specs = (
        P("section", "batch", "tensor", None),
        P("section", None, "tensor"),
        P("section", "tensor"),
        P("section", None, "tensor"),
        P("section", None, "tensor"),
        P("section", "tensor"),
        P("section", "tensor", None),
        P("section", None),
        P("section", None),
        P("section", None),
        P("section", None, "tensor"),
        P("section", "tensor"),
        P("section", "tensor", None),
        P("section", None),
        P("section", None),
        P("section", None),
    )
    return jax.shard_map(shards, mesh=mesh, in_specs=in_specs, out_specs=out_specs, check_vma=False)
```

time: 1090 us -> 623 us (0.57)
  the two profiles are of different devices: /device:TPU:11 before, /device:TPU:1 now
where the time goes in v1:
time: 623 us; the launch traced here: 614 us
  waiting for transfers between devices  304 us (49%)
  starting transfers between devices  101 us (16%)
  Pallas kernels  87.8 us (14%)
  other arithmetic  56.1 us (9%)
  local copies, waits for them, and re-layouts  48.9 us (8%)
  matrix products  14.6 us (2%)
    ppermute x20, waiting for transfers between devices, send(): return lax.ppermute(rows, 'batch', pairs)  187 us
    ppermute x19, waiting for transfers between devices, swap(): return lax.ppermute(block, axis, [(0, 1), (1, 0)])  95.3 us
    pallas_call x8, Pallas kernels, call(): pl.pallas_call(kernel, out_shape=[jax.ShapeDtypeStruct(s, t) for s, t in...  87.8 us
    ppermute x20, starting transfers between devices, send(): return lax.ppermute(rows, 'batch', pairs)  41.2 us
    ppermute x19, starting transfers between devices, swap(): return lax.ppermute(block, axis, [(0, 1), (1, 0)])  26.6 us
    unnamed x124, local copies, waits for them, and re-layouts  26.3 us
    ppermute x6, waiting for transfers between devices, across(): lax.ppermute(block, ('section', 'tensor'), [(a[0] * 2 + a[1], b[0] * 2 +...  20.6 us
    ppermute x2, starting transfers between devices, exchange(): far_one = lax.ppermute(sum_one, 'section', [(1, 0)])  15.4 us
  transfers between devices with their start and end apart: 51, of which 19 were waited for; matrix products, arithmetic and copies ran while one was open for 14% of the time, Pallas kernels for 4%

profile of v1, /device:TPU:1, one launch (start us, length us, event | category | flops | bytes accessed | tf_op | source)
XLA Modules:
  0.0 613.9 jit_solution(5105947759902504860)
XLA Ops:
  1.3 2.1 slice_bitcast_fusion.5
  4.6 1.9 collective-permute-start.4
  9.1 2.8 concatenate.59
  16.0 8.6 %collective-permute-start.5 = (bf16[768,384]{1,0:T(8,128)(2,1)S(1)}, bf16[768,384]{1,0:T(8,128)(2,1)}, u32[]{:S(2)}, u32[]{:S(2)}) collective-permute-start(bf16[768,384]{1,0:T(8,128)(2,1)S(1)} %bitcast.67), channel_id=1, source_target_pairs={{0,16},{16,0},{1,17},{17,1},{2,18},{18,2},{3,19},{19,3},{4,20},{20... | collective-permute-start | bytes 1769480 | tf_op jit(solution)/shard_map/ppermute | solution.py:436
  24.6 3.5 collective-permute-done.2.peer_b
  32.1 12.0 %shard_map.288 = (bf16[512,768]{1,0:T(8,128)(2,1)}, bf16[512,384]{1,0:T(8,128)(2,1)}, bf16[512,384]{1,0:T(8,128)(2,1)}, bf16[512,384]{1,0:T(8,128)(2,1)}, bf16[6...) custom-call(s32[6]{0:T(128)} %pad_add_fusion.flags, ...), custom_call_target="tpu_custom_call" | custom-call | flops 1610612736 | bytes 8388608 | tf_op jit(solution)/shard_map/pallas_call | solution.py:397
  44.1 1.7 collective-permute-start.8
  45.8 17.9 %collective-permute-done.8.part_b = bf16[512,768]{1,0:T(8,128)(2,1)S(1)} collective-permute-done((bf16[512,768]{1,0:T(8,128)(2,1)}, bf16[512,768]{1,0:T(8,128)(2,1)S(1)}, u32[]{:S(2)}, u32[]{:S(2)}) %collective-permute-start.8) | collective-permute-done | bytes 786464 | tf_op jit(solution)/shard_map/ppermute | solution.py:436
  65.4 8.6 %shard_map.289 = (f32[512,768]{1,0:T(8,128)}, f32[512,1]{1,0:T(8,128)}, bf16[512,768]{1,0:T(8,128)(2,1)}, bf16[512,1536]{1,0:T(8,128)(2,1)}, bf16[512,1536]{1,0:T(8,128)(2,1)}, /*index=5*/bf16[512,768]{1,0:T(8,128)(2,1)}) custom-call(s32[6]{0:T(128)} %pad_add_fusion.flags, bf16[512,768]{1,0:T(8,128)(2,1)} %get-tuple-element.69.x, ...), custom_call_target="tpu_custom_call" | custom-call | flops 2415919104 | bytes 8388608 | tf_op jit(solution)/shard_map/pallas_call | solution.py:397
  75.2 17.2 %collective-permute-done.11.part_b = bf16[512,768]{1,0:T(8,128)(2,1)S(1)} collective-permute-done((bf16[512,768]{1,0:T(8,128)(2,1)}, bf16[512,768]{1,0:T(8,128)(2,1)S(1)}, u32[]{:S(2)}, u32[]{:S(2)}) %collective-permute-start.11) | collective-permute-done | bytes 786464 | tf_op jit(solution)/shard_map/ppermute | solution.py:436
  93.3 13.2 %shard_map.290 = (f32[512,768]{1,0:T(8,128)}, f32[512,1]{1,0:T(8,128)}, bf16[512,768]{1,0:T(8,128)(2,1)}, bf16[512,384]{1,0:T(8,128)(2,1)}, bf16[512,384]{1,0:T(...) custom-call(s32[6]{0:T(128)} %pad_add_fusion.flags, ...), custom_call_target="tpu_custom_call" | custom-call | flops 1610612736 | bytes 8388608 | tf_op jit(solution)/shard_map/pallas_call | solution.py:397
  107.5 16.6 %collective-permute-done.12.part_b = bf16[512,768]{1,0:T(8,128)(2,1)S(1)} collective-permute-done((bf16[512,768]{1,0:T(8,128)(2,1)}, bf16[512,768]{1,0:T(8,128)(2,1)S(1)}, u32[]{:S(2)}, u32[]{:S(2)}) %collective-permute-start.12) | collective-permute-done | bytes 786464 | tf_op jit(solution)/shard_map/ppermute | solution.py:436
  125.0 8.6 %shard_map.291 = (f32[512,768]{1,0:T(8,128)}, f32[512,1]{1,0:T(8,128)}, bf16[512,768]{1,0:T(8,128)(2,1)}, bf16[512,1536]{1,0:T(8,128)(2,1)}, bf16[512,1536]{1,0:T(8,128)(2,1)}, /*index=5*/bf16[512,768]{1,0:T(8,128)(2,1)}) custom-call(s32[6]{0:T(128)} %pad_add_fusion.flags, bf16[512,768]{1,0:T(8,128)(2,1)} %get-tuple-element.73.x, ...), custom_call_target="tpu_custom_call" | custom-call | flops 2415919104 | bytes 8388608 | tf_op jit(solution)/shard_map/pallas_call | solution.py:397
  134.2 5.1 collective-permute-start.14
  139.4 2.5 collective-permute-start.15
  143.2 14.1 %collective-permute-done.15.peer_a = bf16[256,768]{1,0:T(8,128)(2,1)S(1)} collective-permute-done((bf16[256,768]{1,0:T(8,128)(2,1)}, bf16[256,768]{1,0:T(8,128)(2,1)S(1)}, u32[]{:S(2)}, u32[]{:S(2)}) %collective-permute-start.15) | collective-permute-done | bytes 393248 | tf_op jit(solution)/shard_map/ppermute | solution.py:440
  157.3 2.9 collective-permute-done.16.peer_b
  161.3 9.6 %shard_map.292 = (bf16[512,768]{1,0:T(8,128)(2,1)}, f32[512,768]{1,0:T(8,128)}, bf16[512,768]{1,0:T(8,128)(2,1)}, bf16[512,1536]{1,0:T(8,128)(2,1)}, bf16[512,768]{1,0:T(8,128)(2,1)}, /*index=5*/f32[8,768]{1,0:T(8,128)}) custom-call(s32[6]{0:T(128)} %pad_add_fusion.flags, f32[512,768]{1,0:T(8,128)} %get-tuple-element.75.normal_one, ...), custom_call_target="tpu_custom_call" | custom-call | flops 2415919104 | bytes 8388608 | tf_op jit(solution)/shard_map/pallas_call | solution.py:397
  171.8 16.4 %collective-permute-done.17.part_b = bf16[512,768]{1,0:T(8,128)(2,1)S(1)} collective-permute-done((bf16[512,768]{1,0:T(8,128)(2,1)}, bf16[512,768]{1,0:T(8,128)(2,1)S(1)}, u32[]{:S(2)}, u32[]{:S(2)}) %collective-permute-start.17) | collective-permute-done | bytes 786464 | tf_op jit(solution)/shard_map/ppermute | solution.py:436
  189.1 13.1 %shard_map.293 = (f32[512,768]{1,0:T(8,128)}, bf16[512,768]{1,0:T(8,128)(2,1)}, bf16[512,1152]{1,0:T(8,128)(2,1)}, bf16[512,768]{1,0:T(8,128)(2,1)}, f32[8,768]{1,0:T(8,128)}) custom-call(s32[6]{0:T(128)} %pad_add_fusion.flags, f32[512,768]{1,0:T(8,128)} %get-tuple-element.78.g2, bf16[512,768]{1,0:T(8,128)(2,1)} %get-tuple-element.79.part_a, ...), custom_call_target="tpu_custom_call" | custom-call | flops 2013265920 | bytes 8388608 | tf_op jit(solution)/shard_map/pallas_call | solution.py:397
  204.9 13.8 %collective-permute-done.18.part_b = bf16[512,768]{1,0:T(8,128)(2,1)S(1)} collective-permute-done((bf16[512,768]{1,0:T(8,128)(2,1)}, bf16[512,768]{1,0:T(8,128)(2,1)S(1)}, u32[]{:S(2)}, u32[]{:S(2)}) %collective-permute-start.18) | collective-permute-done | bytes 786464 | tf_op jit(solution)/shard_map/ppermute | solution.py:436
  219.5 9.6 %shard_map.294 = (f32[512,768]{1,0:T(8,128)}, bf16[512,768]{1,0:T(8,128)(2,1)}, bf16[512,1536]{1,0:T(8,128)(2,1)}, bf16[512,768]{1,0:T(8,128)(2,1)}, f32[8,768]{1,0:T(8,128)}) custom-call(s32[6]{0:T(128)} %pad_add_fusion.flags, f32[512,768]{1,0:T(8,128)} %get-tuple-element.87.g1, bf16[512,768]{1,0:T(8,128)(2,1)} %get-tuple-element.88.part_a, ...), custom_call_target="tpu_custom_call" | custom-call | flops 2415919104 | bytes 8388608 | tf_op jit(solution)/shard_map/pallas_call | solution.py:397
  229.9 2.7 convolution_convert_fusion.2
  232.6 1.7 pad_maximum_fusion.2
  234.3 4.1 collective-permute-start.37
  238.4 3.2 convolution_convert_fusion.1
  243.1 3.3 collective-permute-done.37
  246.4 3.1 fusion
  250.8 1.8 collective-permute-start.45
  259.0 4.6 collective-permute-start.38
  263.6 8.6 %collective-permute-done.19.part_b = bf16[512,768]{1,0:T(8,128)(2,1)S(1)} collective-permute-done((bf16[512,768]{1,0:T(8,128)(2,1)S(1)}, bf16[512,768]{1,0:T(8,128)(2,1)S(1)}, u32[]{:S(2)}, u32[]{:S(2)}) %collective-permute-start.19) | collective-permute-done | bytes 786464 | tf_op jit(solution)/shard_map/ppermute | solution.py:436
  273.1 13.2 %shard_map.295 = (f32[512,768]{1,0:T(8,128)}, bf16[512,768]{1,0:T(8,128)(2,1)}, bf16[512,1152]{1,0:T(8,128)(2,1)}, bf16[512,768]{1,0:T(8,128)(2,1)}, f32[8,768]{1,0:T(8,128)}) custom-call(s32[6]{0:T(128)} %pad_add_fusion.flags, f32[512,768]{1,0:T(8,128)} %get-tuple-element.92.g2, bf16[512,768]{1,0:T(8,128)(2,1)} %get-tuple-element.93.part_a, ...), custom_call_target="tpu_custom_call" | custom-call | flops 2013265920 | bytes 8388608 | tf_op jit(solution)/shard_map/pallas_call | solution.py:397
  286.3 2.7 dynamic-slice_add_fusion
  289.1 4.3 collective-permute-start.46
  295.2 1.8 fusion.13
  297.1 1.7 collective-permute-start.23
  298.8 41.1 %collective-permute-done.46 = bf16[784,768]{1,0:T(8,128)(2,1)} collective-permute-done((bf16[784,768]{1,0:T(8,128)(2,1)}, bf16[784,768]{1,0:T(8,128)(2,1)}, u32[]{:S(2)}, u32[]{:S(2)}) %collective-permute-start.46) | collective-permute-done | bytes 1204256 | tf_op jit(solution)/shard_map/ppermute | solution.py:450
  339.9 1.9 add.117
  343.1 7.7 %collective-permute-start.30 = (bf16[800,768]{1,0:T(8,128)(2,1)}, bf16[800,768]{1,0:T(8,128)(2,1)}, u32[]{:S(2)}, u32[]{:S(2)}) collective-permute-start(bf16[800,768]{1,0:T(8,128)(2,1)} %get-tuple-element.172), channel_id=1, source_target_pairs={{0,4},{2,6},{12,8},{14,10},{1,5},{3,7},{13,9},{15,11},{16,20},{18,... | collective-permute-start | bytes 3686408 | tf_op jit(solution)/shard_map/ppermute | solution.py:450
  351.3 2.3 add.109
  361.4 13.8 %collective-permute-done.30 = bf16[800,768]{1,0:T(8,128)(2,1)} collective-permute-done((bf16[800,768]{1,0:T(8,128)(2,1)}, bf16[800,768]{1,0:T(8,128)(2,1)}, u32[]{:S(2)}, u32[]{:S(2)}) %collective-permute-start.30) | collective-permute-done | bytes 1228832 | tf_op jit(solution)/shard_map/ppermute | solution.py:450
  375.3 2.1 add.104
  378.6 4.9 collective-permute-start.25
  383.6 2.7 dynamic-slice_add_fusion.1
  386.3 1.9 collective-permute-start.40
  390.6 3.0 collective-permute-done.25
  396.3 3.9 collective-permute-done.48
  402.1 2.0 dynamic-slice_add_fusion.2
  407.5 3.0 add.112
  410.6 1.7 collective-permute-start.41
  417.4 30.7 %collective-permute-done.27 = bf16[400,768]{1,0:T(8,128)(2,1)} collective-permute-done((bf16[400,768]{1,0:T(8,128)(2,1)S(1)}, bf16[400,768]{1,0:T(8,128)(2,1)}, u32[]{:S(2)}, u32[]{:S(2)}) %collective-permute-start.27) | collective-permute-done | bytes 614432 | tf_op jit(solution)/shard_map/ppermute | solution.py:450
  453.9 1.8 broadcast_select_fusion.6
  457.4 4.5 collective-permute-done.28
  463.4 6.7 %collective-permute-start.36 = (bf16[800,768]{1,0:T(8,128)(2,1)S(1)}, bf16[800,768]{1,0:T(8,128)(2,1)S(1)}, u32[]{:S(2)}, u32[]{:S(2)}) collective-permute-start(bf16[800,768]{1,0:T(8,128)(2,1)S(1)} %pad_maximum_fusion.18), channel_id=1, source_target_pairs={{16,0},{17,1},{18,2},{19,3},{20,4},{21,5},{22,6},{23,7},{24,8},{25... | collective-permute-start | bytes 3686408 | tf_op jit(solution)/shard_map/ppermute | solution.py:678
  473.2 89.6 %collective-permute-done.34 = bf16[800,768]{1,0:T(8,128)(2,1)S(1)} collective-permute-done((bf16[800,768]{1,0:T(8,128)(2,1)S(1)}, bf16[800,768]{1,0:T(8,128)(2,1)S(1)}, u32[]{:S(2)}, u32[]{:S(2)}) %collective-permute-start.34) | collective-permute-done | bytes 1228832 | tf_op jit(solution)/shard_map/ppermute | solution.py:450
  566.6 4.0 select_convert_fusion
  570.6 8.7 %collective-permute-start.43 = (bf16[1568,768]{1,0:T(8,128)(2,1)}, bf16[1568,768]{1,0:T(8,128)(2,1)}, u32[]{:S(2)}, u32[]{:S(2)}) collective-permute-start(bf16[1568,768]{1,0:T(8,128)(2,1)} %get-tuple-element.139), channel_id=1, source_target_pairs={{16,0},{17,1},{18,2},{19,3},{20,4},{21,5},{22,6},{23,7},{24,8},{25... | collective-permute-start | bytes 7225352 | tf_op jit(solution)/shard_map/ppermute | solution.py:678
  580.9 2.7 copy.35
  583.5 1.7 select_convert_fusion.2
  587.5 2.7 copy.33
  590.1 2.7 copy.34
  598.3 4.8 slice_bitcast_fusion
  603.1 4.3 convert_bitcast_fusion
  607.4 6.1 copy.36
  (242 shorter events, 90.2 us)
Async XLA Ops:
  0.6 28.5 %copy-start = (s32[2,4]{1,0:T(2,128)S(1)}, s32[2,4]{1,0:T(2,128)}, u32[]{:S(2)}) copy-start(s32[2,4]{1,0:T(2,128)} %param.18) | copy-start | bytes 100
  0.7 15.3 %copy-start.7 = (bf16[1,768,384]{2,1,0:T(8,128)(2,1)S(1)}, bf16[1,768,384]{2,1,0:T(8,128)(2,1)}, u32[]{:S(2)}) copy-start(bf16[1,768,384]{2,1,0:T(8,128)(2,1)} %param.21) | copy-start | bytes 1769476
  0.7 62.9 %collective-permute-start.9 = (bf16[768,1536]{1,0:T(8,128)(2,1)}, bf16[768,1536]{1,0:T(8,128)(2,1)S(1)}, u32[]{:S(2)}, u32[]{:S(2)}) collective-permute-start(bf16[768,1536]{1,0:T(8,128)(2,1)} %bitcast.48), channel_id=1, source_target_pairs={{0,16},{16,0},{1,17},{17,1},{2,18},{18,2},{3,19},{19,3},{4,20},{20... | collective-permute-start | bytes 7077896 | tf_op jit(solution)/shard_map/ppermute | solution.py:436
  0.8 62.8 %collective-permute-start.10 = (bf16[1536,768]{1,0:T(8,128)(2,1)}, bf16[1536,768]{1,0:T(8,128)(2,1)}, u32[]{:S(2)}, u32[]{:S(2)}) collective-permute-start(bf16[1536,768]{1,0:T(8,128)(2,1)} %bitcast.53), channel_id=1, source_target_pairs={{0,16},{16,0},{1,17},{17,1},{2,18},{18,2},{3,19},{19,3},{4,20},{20... | collective-permute-start | bytes 7077896 | tf_op jit(solution)/shard_map/ppermute | solution.py:436
  3.3 11.3 %collective-permute-start = (bf16[256,768]{1,0:T(8,128)(2,1)}, bf16[256,768]{1,0:T(8,128)(2,1)}, u32[]{:S(2)}, u32[]{:S(2)}) collective-permute-start(bf16[256,768]{1,0:T(8,128)(2,1)} %get-tuple-element.164.own), channel_id=1, source_target_pairs={{0,16},{1,17},{2,18},{3,19},{4,20},{5,21},{6,22},{7,23},{8,24},{9,... | collective-permute-start | bytes 1179656 | tf_op jit(solution)/shard_map/ppermute | solution.py:440
  4.6 23.8 %collective-permute-start.4 = (bf16[768,384]{1,0:T(8,128)(2,1)S(1)}, bf16[768,384]{1,0:T(8,128)(2,1)}, u32[]{:S(2)}, u32[]{:S(2)}) collective-permute-start(bf16[768,384]{1,0:T(8,128)(2,1)S(1)} %bitcast.62), channel_id=1, source_target_pairs={{0,16},{16,0},{1,17},{17,1},{2,18},{18,2},{3,19},{19,3},{4,20},{20... | collective-permute-start | bytes 1769480 | tf_op jit(solution)/shard_map/ppermute | solution.py:436
  11.9 1.4 collective-permute-start.3
  14.0 2.0 collective-permute-start.1
  14.7 13.4 %collective-permute-start.2 = (bf16[256,768]{1,0:T(8,128)(2,1)}, bf16[256,768]{1,0:T(8,128)(2,1)S(1)}, u32[]{:S(2)}, u32[]{:S(2)}) collective-permute-start(bf16[256,768]{1,0:T(8,128)(2,1)} %get-tuple-element.164.own), channel_id=1, source_target_pairs={{0,17},{1,16},{2,19},{3,18},{4,21},{5,20},{6,23},{7,22},{8,25},{9,... | collective-permute-start | bytes 1179656 | tf_op jit(solution)/shard_map/ppermute | solution.py:440
  16.0 12.5 %copy-start.30 = (bf16[256,768]{1,0:T(8,128)(2,1)}, bf16[256,768]{1,0:T(8,128)(2,1)S(1)}, u32[]{:S(2)}) copy-start(bf16[256,768]{1,0:T(8,128)(2,1)S(1)} %collective-permute-done.1.peer_a) | copy-start | bytes 1179652
  16.0 15.3 %collective-permute-start.5 = (bf16[768,384]{1,0:T(8,128)(2,1)S(1)}, bf16[768,384]{1,0:T(8,128)(2,1)}, u32[]{:S(2)}, u32[]{:S(2)}) collective-permute-start(bf16[768,384]{1,0:T(8,128)(2,1)S(1)} %bitcast.67), channel_id=1, source_target_pairs={{0,16},{16,0},{1,17},{17,1},{2,18},{18,2},{3,19},{19,3},{4,20},{20... | collective-permute-start | bytes 1769480 | tf_op jit(solution)/shard_map/ppermute | solution.py:436
  28.1 3.1 collective-permute-start.6
  28.8 2.4 collective-permute-start.7
  44.1 19.6 %collective-permute-start.8 = (bf16[512,768]{1,0:T(8,128)(2,1)}, bf16[512,768]{1,0:T(8,128)(2,1)S(1)}, u32[]{:S(2)}, u32[]{:S(2)}) collective-permute-start(bf16[512,768]{1,0:T(8,128)(2,1)} %get-tuple-element.70.part_a), channel_id=1, source_target_pairs={{0,1},{1,0},{2,3},{3,2},{4,5},{5,4},{6,7},{7,6},{8,9},{9,8},{10,11... | collective-permute-start | bytes 2359304 | tf_op jit(solution)/shard_map/ppermute | solution.py:436
  73.9 18.5 %collective-permute-start.11 = (bf16[512,768]{1,0:T(8,128)(2,1)}, bf16[512,768]{1,0:T(8,128)(2,1)S(1)}, u32[]{:S(2)}, u32[]{:S(2)}) collective-permute-start(bf16[512,768]{1,0:T(8,128)(2,1)} %get-tuple-element.72.part_a), channel_id=1, source_target_pairs={{0,1},{1,0},{2,3},{3,2},{4,5},{5,4},{6,7},{7,6},{8,9},{9,8},{10,11... | collective-permute-start | bytes 2359304 | tf_op jit(solution)/shard_map/ppermute | solution.py:436
  106.5 17.6 %collective-permute-start.12 = (bf16[512,768]{1,0:T(8,128)(2,1)}, bf16[512,768]{1,0:T(8,128)(2,1)S(1)}, u32[]{:S(2)}, u32[]{:S(2)}) collective-permute-start(bf16[512,768]{1,0:T(8,128)(2,1)} %get-tuple-element.74.part_a), channel_id=1, source_target_pairs={{0,1},{1,0},{2,3},{3,2},{4,5},{5,4},{6,7},{7,6},{8,9},{9,8},{10,11... | collective-permute-start | bytes 2359304 | tf_op jit(solution)/shard_map/ppermute | solution.py:436
  133.6 26.7 %collective-permute-start.13 = (bf16[512,768]{1,0:T(8,128)(2,1)}, bf16[512,768]{1,0:T(8,128)(2,1)S(1)}, u32[]{:S(2)}, u32[]{:S(2)}) collective-permute-start(bf16[512,768]{1,0:T(8,128)(2,1)} %get-tuple-element.76.part_a), channel_id=1, source_target_pairs={{0,1},{1,0},{2,3},{3,2},{4,5},{5,4},{6,7},{7,6},{8,9},{9,8},{10,11... | collective-permute-start | bytes 2359304 | tf_op jit(solution)/shard_map/ppermute | solution.py:436
  134.2 8.9 %collective-permute-start.14 = (bf16[256,768]{1,0:T(8,128)(2,1)S(1)}, bf16[256,768]{1,0:T(8,128)(2,1)S(1)}, u32[]{:S(2)}, u32[]{:S(2)}) collective-permute-start(bf16[256,768]{1,0:T(8,128)(2,1)S(1)} %copy-done.14), channel_id=1, source_target_pairs={{16,0},{17,1},{18,2},{19,3},{20,4},{21,5},{22,6},{23,7},{24,8},{25... | collective-permute-start | bytes 1179656 | tf_op jit(solution)/shard_map/ppermute | solution.py:440
  139.4 17.9 %collective-permute-start.15 = (bf16[256,768]{1,0:T(8,128)(2,1)}, bf16[256,768]{1,0:T(8,128)(2,1)S(1)}, u32[]{:S(2)}, u32[]{:S(2)}) collective-permute-start(bf16[256,768]{1,0:T(8,128)(2,1)} %get-tuple-element.164.own), channel_id=1, source_target_pairs={{16,17},{17,16},{18,19},{19,18},{20,21},{21,20},{22,23},{23,22},{2... | collective-permute-start | bytes 1179656 | tf_op jit(solution)/shard_map/ppermute | solution.py:440
  141.8 18.4 %collective-permute-start.16 = (bf16[256,768]{1,0:T(8,128)(2,1)S(1)}, bf16[256,768]{1,0:T(8,128)(2,1)S(1)}, u32[]{:S(2)}, u32[]{:S(2)}) collective-permute-start(bf16[256,768]{1,0:T(8,128)(2,1)S(1)} %copy-done.14), channel_id=1, source_target_pairs={{16,1},{17,0},{18,3},{19,2},{20,5},{21,4},{22,7},{23,6},{24,9},{25... | collective-permute-start | bytes 1179656 | tf_op jit(solution)/shard_map/ppermute | solution.py:440
  143.2 17.1 %copy-start.33 = (bf16[256,768]{1,0:T(8,128)(2,1)}, bf16[256,768]{1,0:T(8,128)(2,1)S(1)}, u32[]{:S(2)}) copy-start(bf16[256,768]{1,0:T(8,128)(2,1)S(1)} %collective-permute-done.14.far) | copy-start | bytes 1179652
  170.9 17.3 %collective-permute-start.17 = (bf16[512,768]{1,0:T(8,128)(2,1)}, bf16[512,768]{1,0:T(8,128)(2,1)S(1)}, u32[]{:S(2)}, u32[]{:S(2)}) collective-permute-start(bf16[512,768]{1,0:T(8,128)(2,1)} %get-tuple-element.79.part_a), channel_id=1, source_target_pairs={{0,1},{1,0},{2,3},{3,2},{4,5},{5,4},{6,7},{7,6},{8,9},{9,8},{10,11... | collective-permute-start | bytes 2359304 | tf_op jit(solution)/shard_map/ppermute | solution.py:436
  189.1 14.3 %copy-start.38 = (f32[8,768]{1,0:T(8,128)S(1)}, f32[8,768]{1,0:T(8,128)}, u32[]{:S(2)}) copy-start(f32[8,768]{1,0:T(8,128)} %get-tuple-element.121) | copy-start | bytes 73732
  189.1 14.3 %copy-start.43 = (bf16[512,1536]{1,0:T(8,128)(2,1)S(1)}, bf16[512,1536]{1,0:T(8,128)(2,1)}, u32[]{:S(2)}) copy-start(bf16[512,1536]{1,0:T(8,128)(2,1)} %get-tuple-element.117) | copy-start | bytes 4718596
  189.1 14.3 %copy-start.44 = (bf16[512,1536]{1,0:T(8,128)(2,1)S(1)}, bf16[512,1536]{1,0:T(8,128)(2,1)}, u32[]{:S(2)}) copy-start(bf16[512,1536]{1,0:T(8,128)(2,1)} %get-tuple-element.118) | copy-start | bytes 4718596
  189.1 14.3 %copy-start.50 = (bf16[512,768]{1,0:T(8,128)(2,1)S(1)}, bf16[512,768]{1,0:T(8,128)(2,1)}, u32[]{:S(2)}) copy-start(bf16[512,768]{1,0:T(8,128)(2,1)} %get-tuple-element.120) | copy-start | bytes 2359300
  189.1 14.3 %copy-start.52 = (bf16[512,768]{1,0:T(8,128)(2,1)S(1)}, bf16[512,768]{1,0:T(8,128)(2,1)}, u32[]{:S(2)}) copy-start(bf16[512,768]{1,0:T(8,128)(2,1)} %get-tuple-element.119) | copy-start | bytes 2359300
  202.2 16.4 %collective-permute-start.18 = (bf16[512,768]{1,0:T(8,128)(2,1)}, bf16[512,768]{1,0:T(8,128)(2,1)S(1)}, u32[]{:S(2)}, u32[]{:S(2)}) collective-permute-start(bf16[512,768]{1,0:T(8,128)(2,1)} %get-tuple-element.88.part_a), channel_id=1, source_target_pairs={{0,1},{1,0},{2,3},{3,2},{4,5},{5,4},{6,7},{7,6},{8,9},{9,8},{10,11... | collective-permute-start | bytes 2359304 | tf_op jit(solution)/shard_map/ppermute | solution.py:436
  234.3 12.1 %collective-permute-start.37 = (bf16[1568,768]{1,0:T(8,128)(2,1)}, bf16[1568,768]{1,0:T(8,128)(2,1)}, u32[]{:S(2)}, u32[]{:S(2)}) collective-permute-start(bf16[1568,768]{1,0:T(8,128)(2,1)} %get-tuple-element.170), channel_id=1, source_target_pairs={{0,16},{16,0},{1,17},{17,1},{2,18},{18,2},{3,19},{19,3},{4,20},{20... | collective-permute-start | bytes 7225352 | tf_op jit(solution)/shard_map/ppermute | solution.py:436
  238.4 8.0 %collective-permute-start.44 = (bf16[1568,768]{1,0:T(8,128)(2,1)S(1)}, bf16[1568,768]{1,0:T(8,128)(2,1)}, u32[]{:S(2)}, u32[]{:S(2)}) collective-permute-start(bf16[1568,768]{1,0:T(8,128)(2,1)S(1)} %get-tuple-element.171), channel_id=1, source_target_pairs={{0,16},{16,0},{1,17},{17,1},{2,18},{18,2},{3,19},{19,3},{4,20},{20... | collective-permute-start | bytes 7225352 | tf_op jit(solution)/shard_map/ppermute | solution.py:436
  250.8 35.6 %collective-permute-start.45 = (bf16[784,768]{1,0:T(8,128)(2,1)}, bf16[784,768]{1,0:T(8,128)(2,1)}, u32[]{:S(2)}, u32[]{:S(2)}) collective-permute-start(bf16[784,768]{1,0:T(8,128)(2,1)} %constant_dynamic-slice_fusion), channel_id=1, source_target_pairs={{0,2},{2,0},{4,6},{6,4},{8,10},{10,8},{12,14},{14,12},{1,3},{3,1},... | collective-permute-start | bytes 3612680 | tf_op jit(solution)/shard_map/ppermute | solution.py:450
  253.7 18.5 %collective-permute-start.19 = (bf16[512,768]{1,0:T(8,128)(2,1)S(1)}, bf16[512,768]{1,0:T(8,128)(2,1)S(1)}, u32[]{:S(2)}, u32[]{:S(2)}) collective-permute-start(bf16[512,768]{1,0:T(8,128)(2,1)S(1)} %copy-done.15), channel_id=1, source_target_pairs={{0,1},{1,0},{2,3},{3,2},{4,5},{5,4},{6,7},{7,6},{8,9},{9,8},{10,11... | collective-permute-start | bytes 2359304 | tf_op jit(solution)/shard_map/ppermute | solution.py:436
  255.4 39.1 %collective-permute-start.29 = (bf16[800,768]{1,0:T(8,128)(2,1)}, bf16[800,768]{1,0:T(8,128)(2,1)S(1)}, u32[]{:S(2)}, u32[]{:S(2)}) collective-permute-start(bf16[800,768]{1,0:T(8,128)(2,1)} %pad_maximum_fusion.9), channel_id=1, source_target_pairs={{0,16},{16,0},{1,17},{17,1},{2,18},{18,2},{3,19},{19,3},{4,20},{20... | collective-permute-start | bytes 3686408 | tf_op jit(solution)/shard_map/ppermute | solution.py:436
  259.0 92.2 %collective-permute-start.38 = (bf16[1568,768]{1,0:T(8,128)(2,1)S(1)}, bf16[1568,768]{1,0:T(8,128)(2,1)}, u32[]{:S(2)}, u32[]{:S(2)}) collective-permute-start(bf16[1568,768]{1,0:T(8,128)(2,1)S(1)} %get-tuple-element.168), channel_id=1, source_target_pairs={{0,4},{2,6},{12,8},{14,10},{1,5},{3,7},{13,9},{15,11},{16,20},{18,... | collective-permute-start | bytes 7225352 | tf_op jit(solution)/shard_map/ppermute | solution.py:450
  289.1 50.8 %collective-permute-start.46 = (bf16[784,768]{1,0:T(8,128)(2,1)}, bf16[784,768]{1,0:T(8,128)(2,1)}, u32[]{:S(2)}, u32[]{:S(2)}) collective-permute-start(bf16[784,768]{1,0:T(8,128)(2,1)} %dynamic-slice_add_fusion), channel_id=1, source_target_pairs={{0,4},{2,6},{12,8},{14,10},{1,5},{3,7},{13,9},{15,11},{16,20},{18,... | collective-permute-start | bytes 3612680 | tf_op jit(solution)/shard_map/ppermute | solution.py:450
  297.1 59.4 %collective-permute-start.23 = (bf16[800,768]{1,0:T(8,128)(2,1)}, bf16[800,768]{1,0:T(8,128)(2,1)}, u32[]{:S(2)}, u32[]{:S(2)}) collective-permute-start(bf16[800,768]{1,0:T(8,128)(2,1)} %get-tuple-element.173), channel_id=1, source_target_pairs={{0,16},{16,0},{1,17},{17,1},{2,18},{18,2},{3,19},{19,3},{4,20},{20... | collective-permute-start | bytes 3686408 | tf_op jit(solution)/shard_map/ppermute | solution.py:436
  298.8 43.7 %copy-start.48 = (bf16[512,1152]{1,0:T(8,128)(2,1)S(1)}, bf16[512,1152]{1,0:T(8,128)(2,1)}, u32[]{:S(2)}) copy-start(bf16[512,1152]{1,0:T(8,128)(2,1)} %get-tuple-element.104) | copy-start | bytes 3538948
  298.8 43.8 %copy-start.54 = (bf16[512,768]{1,0:T(8,128)(2,1)S(1)}, bf16[512,768]{1,0:T(8,128)(2,1)}, u32[]{:S(2)}) copy-start(bf16[512,768]{1,0:T(8,128)(2,1)} %get-tuple-element.106) | copy-start | bytes 2359300
  298.8 43.8 %copy-start.57 = (bf16[512,384]{1,0:T(8,128)(2,1)S(1)}, bf16[512,384]{1,0:T(8,128)(2,1)}, u32[]{:S(2)}) copy-start(bf16[512,384]{1,0:T(8,128)(2,1)} %get-tuple-element.105) | copy-start | bytes 1179652
  341.8 17.0 %collective-permute-start.47 = (bf16[784,768]{1,0:T(8,128)(2,1)S(1)}, bf16[784,768]{1,0:T(8,128)(2,1)S(1)}, u32[]{:S(2)}, u32[]{:S(2)}) collective-permute-start(bf16[784,768]{1,0:T(8,128)(2,1)S(1)} %add.117), channel_id=1, source_target_pairs={{4,8},{6,10},{8,4},{10,6},{5,9},{7,11},{9,5},{11,7},{20,24},{22,26... | collective-permute-start | bytes 3612680 | tf_op jit(solution)/shard_map/ppermute | solution.py:450
  343.1 32.2 %collective-permute-start.30 = (bf16[800,768]{1,0:T(8,128)(2,1)}, bf16[800,768]{1,0:T(8,128)(2,1)}, u32[]{:S(2)}, u32[]{:S(2)}) collective-permute-start(bf16[800,768]{1,0:T(8,128)(2,1)} %get-tuple-element.172), channel_id=1, source_target_pairs={{0,4},{2,6},{12,8},{14,10},{1,5},{3,7},{13,9},{15,11},{16,20},{18,... | collective-permute-start | bytes 3686408 | tf_op jit(solution)/shard_map/ppermute | solution.py:450
  354.8 28.8 %collective-permute-start.39 = (bf16[784,768]{1,0:T(8,128)(2,1)}, bf16[784,768]{1,0:T(8,128)(2,1)}, u32[]{:S(2)}, u32[]{:S(2)}) collective-permute-start(bf16[784,768]{1,0:T(8,128)(2,1)} %constant_dynamic-slice_fusion.1), channel_id=1, source_target_pairs={{4,8},{6,10},{8,4},{10,6},{5,9},{7,11},{9,5},{11,7},{20,24},{22,26... | collective-permute-start | bytes 3612680 | tf_op jit(solution)/shard_map/ppermute | solution.py:450
  358.1 19.2 %collective-permute-start.24 = (bf16[400,768]{1,0:T(8,128)(2,1)S(1)}, bf16[400,768]{1,0:T(8,128)(2,1)}, u32[]{:S(2)}, u32[]{:S(2)}) collective-permute-start(bf16[400,768]{1,0:T(8,128)(2,1)S(1)} %constant_dynamic-slice_fusion.3), channel_id=1, source_target_pairs={{0,2},{2,0},{4,6},{6,4},{8,10},{10,8},{12,14},{14,12},{1,3},{3,1},... | collective-permute-start | bytes 1843208 | tf_op jit(solution)/shard_map/ppermute | solution.py:450
  360.1 40.0 %collective-permute-start.48 = (bf16[784,768]{1,0:T(8,128)(2,1)}, bf16[784,768]{1,0:T(8,128)(2,1)}, u32[]{:S(2)}, u32[]{:S(2)}) collective-permute-start(bf16[784,768]{1,0:T(8,128)(2,1)} %add.118), channel_id=1, source_target_pairs={{4,0},{6,2},{8,12},{10,14},{5,1},{7,3},{9,13},{11,15},{20,16},{22,... | collective-permute-start | bytes 3612680 | tf_op jit(solution)/shard_map/ppermute | solution.py:450
  378.6 15.0 %collective-permute-start.25 = (bf16[400,768]{1,0:T(8,128)(2,1)S(1)}, bf16[400,768]{1,0:T(8,128)(2,1)}, u32[]{:S(2)}, u32[]{:S(2)}) collective-permute-start(bf16[400,768]{1,0:T(8,128)(2,1)S(1)} %dynamic-slice_add_fusion.3), channel_id=1, source_target_pairs={{0,4},{2,6},{12,8},{14,10},{1,5},{3,7},{13,9},{15,11},{16,20},{18,... | collective-permute-start | bytes 1843208 | tf_op jit(solution)/shard_map/ppermute | solution.py:450
  386.3 21.3 %collective-permute-start.40 = (bf16[784,768]{1,0:T(8,128)(2,1)}, bf16[784,768]{1,0:T(8,128)(2,1)}, u32[]{:S(2)}, u32[]{:S(2)}) collective-permute-start(bf16[784,768]{1,0:T(8,128)(2,1)} %dynamic-slice_add_fusion.1), channel_id=1, source_target_pairs={{4,6},{6,4},{8,10},{10,8},{5,7},{7,5},{9,11},{11,9},{20,22},{22,20... | collective-permute-start | bytes 3612680 | tf_op jit(solution)/shard_map/ppermute | solution.py:450
  389.1 13.0 %collective-permute-start.31 = (bf16[400,768]{1,0:T(8,128)(2,1)}, bf16[400,768]{1,0:T(8,128)(2,1)}, u32[]{:S(2)}, u32[]{:S(2)}) collective-permute-start(bf16[400,768]{1,0:T(8,128)(2,1)} %constant_dynamic-slice_fusion.2), channel_id=1, source_target_pairs={{4,8},{6,10},{8,4},{10,6},{5,9},{7,11},{9,5},{11,7},{20,24},{22,26... | collective-permute-start | bytes 1843208 | tf_op jit(solution)/shard_map/ppermute | solution.py:450
  394.8 10.1 %collective-permute-start.26 = (bf16[400,768]{1,0:T(8,128)(2,1)S(1)}, bf16[400,768]{1,0:T(8,128)(2,1)}, u32[]{:S(2)}, u32[]{:S(2)}) collective-permute-start(bf16[400,768]{1,0:T(8,128)(2,1)S(1)} %add.101), channel_id=1, source_target_pairs={{4,8},{6,10},{8,4},{10,6},{5,9},{7,11},{9,5},{11,7},{20,24},{22,26... | collective-permute-start | bytes 1843208 | tf_op jit(solution)/shard_map/ppermute | solution.py:450
  401.6 48.4 %collective-permute-start.49 = (bf16[784,768]{1,0:T(8,128)(2,1)S(1)}, bf16[784,768]{1,0:T(8,128)(2,1)}, u32[]{:S(2)}, u32[]{:S(2)}) collective-permute-start(bf16[784,768]{1,0:T(8,128)(2,1)S(1)} %broadcast_select_fusion.2), channel_id=1, source_target_pairs={{0,2},{2,0},{4,6},{6,4},{8,10},{10,8},{12,14},{14,12},{1,3},{3,1},... | collective-permute-start | bytes 3612680 | tf_op jit(solution)/shard_map/ppermute | solution.py:450
  404.2 10.5 %collective-permute-start.32 = (bf16[400,768]{1,0:T(8,128)(2,1)}, bf16[400,768]{1,0:T(8,128)(2,1)S(1)}, u32[]{:S(2)}, u32[]{:S(2)}) collective-permute-start(bf16[400,768]{1,0:T(8,128)(2,1)} %dynamic-slice_add_fusion.2), channel_id=1, source_target_pairs={{4,6},{6,4},{8,10},{10,8},{5,7},{7,5},{9,11},{11,9},{20,22},{22,20... | collective-permute-start | bytes 1843208 | tf_op jit(solution)/shard_map/ppermute | solution.py:450
  406.1 42.0 %collective-permute-start.27 = (bf16[400,768]{1,0:T(8,128)(2,1)S(1)}, bf16[400,768]{1,0:T(8,128)(2,1)}, u32[]{:S(2)}, u32[]{:S(2)}) collective-permute-start(bf16[400,768]{1,0:T(8,128)(2,1)S(1)} %add.102), channel_id=1, source_target_pairs={{4,0},{6,2},{8,12},{10,14},{5,1},{7,3},{9,13},{11,15},{20,16},{22,... | collective-permute-start | bytes 1843208 | tf_op jit(solution)/shard_map/ppermute | solution.py:450
  410.6 42.0 %collective-permute-start.41 = (bf16[784,768]{1,0:T(8,128)(2,1)}, bf16[784,768]{1,0:T(8,128)(2,1)}, u32[]{:S(2)}, u32[]{:S(2)}) collective-permute-start(bf16[784,768]{1,0:T(8,128)(2,1)} %add.112), channel_id=1, source_target_pairs={{4,8},{6,10},{8,4},{10,6},{5,9},{7,11},{9,5},{11,7},{20,24},{22,26... | collective-permute-start | bytes 3612680 | tf_op jit(solution)/shard_map/ppermute | solution.py:450
  413.3 50.1 %collective-permute-start.21 = (bf16[256,768]{1,0:T(8,128)(2,1)S(1)}, bf16[256,768]{1,0:T(8,128)(2,1)S(1)}, u32[]{:S(2)}, u32[]{:S(2)}) collective-permute-start(bf16[256,768]{1,0:T(8,128)(2,1)S(1)} %constant_dynamic-slice_fusion.4), channel_id=1, source_target_pairs={{0,16},{1,17},{2,18},{3,19},{4,20},{5,21},{6,22},{7,23},{8,24},{9,... | collective-permute-start | bytes 1179656 | tf_op jit(solution)/shard_map/ppermute | solution.py:670
  414.7 36.3 %copy-start.11 = (bf16[784,768]{1,0:T(8,128)(2,1)S(1)}, bf16[784,768]{1,0:T(8,128)(2,1)}, u32[]{:S(2)}) copy-start(bf16[784,768]{1,0:T(8,128)(2,1)} %copy-done.10) | copy-start | bytes 3612676
  414.7 55.4 %collective-permute-start.20 = (bf16[256,768]{1,0:T(8,128)(2,1)S(1)}, bf16[256,768]{1,0:T(8,128)(2,1)S(1)}, u32[]{:S(2)}, u32[]{:S(2)}) collective-permute-start(bf16[256,768]{1,0:T(8,128)(2,1)S(1)} %constant_dynamic-slice_fusion.5), channel_id=1, source_target_pairs={{0,1},{1,0},{2,3},{3,2},{4,5},{5,4},{6,7},{7,6},{8,9},{9,8},{10,11... | collective-permute-start | bytes 1179656 | tf_op jit(solution)/shard_map/ppermute | solution.py:436
  448.1 7.8 %collective-permute-start.33 = (bf16[400,768]{1,0:T(8,128)(2,1)S(1)}, bf16[400,768]{1,0:T(8,128)(2,1)S(1)}, u32[]{:S(2)}, u32[]{:S(2)}) collective-permute-start(bf16[400,768]{1,0:T(8,128)(2,1)S(1)} %add.107), channel_id=1, source_target_pairs={{4,8},{6,10},{8,4},{10,6},{5,9},{7,11},{9,5},{11,7},{20,24},{22,26... | collective-permute-start | bytes 1843208 | tf_op jit(solution)/shard_map/ppermute | solution.py:450
  450.0 11.9 %collective-permute-start.28 = (bf16[400,768]{1,0:T(8,128)(2,1)S(1)}, bf16[400,768]{1,0:T(8,128)(2,1)S(1)}, u32[]{:S(2)}, u32[]{:S(2)}) collective-permute-start(bf16[400,768]{1,0:T(8,128)(2,1)S(1)} %broadcast_select_fusion.9), channel_id=1, source_target_pairs={{0,2},{2,0},{4,6},{6,4},{8,10},{10,8},{12,14},{14,12},{1,3},{3,1},... | collective-permute-start | bytes 1843208 | tf_op jit(solution)/shard_map/ppermute | solution.py:450
  452.6 114.0 %collective-permute-start.50 = (bf16[1568,768]{1,0:T(8,128)(2,1)S(1)}, bf16[1568,768]{1,0:T(8,128)(2,1)S(1)}, u32[]{:S(2)}, u32[]{:S(2)}) collective-permute-start(bf16[1568,768]{1,0:T(8,128)(2,1)S(1)} %pad_maximum_fusion.8), channel_id=1, source_target_pairs={{0,16},{1,17},{2,18},{3,19},{4,20},{5,21},{6,22},{7,23},{8,24},{9,... | collective-permute-start | bytes 7225352 | tf_op jit(solution)/shard_map/ppermute | solution.py:677
  455.9 110.7 %collective-permute-start.42 = (bf16[1568,768]{1,0:T(8,128)(2,1)S(1)}, bf16[1568,768]{1,0:T(8,128)(2,1)S(1)}, u32[]{:S(2)}, u32[]{:S(2)}) collective-permute-start(bf16[1568,768]{1,0:T(8,128)(2,1)S(1)} %pad_maximum_fusion.13), channel_id=1, source_target_pairs={{4,0},{6,2},{8,12},{10,14},{5,1},{7,3},{9,13},{11,15},{20,16},{22,... | collective-permute-start | bytes 7225352 | tf_op jit(solution)/shard_map/ppermute | solution.py:450
  461.9 101.0 %collective-permute-start.34 = (bf16[800,768]{1,0:T(8,128)(2,1)S(1)}, bf16[800,768]{1,0:T(8,128)(2,1)S(1)}, u32[]{:S(2)}, u32[]{:S(2)}) collective-permute-start(bf16[800,768]{1,0:T(8,128)(2,1)S(1)} %pad_maximum_fusion.19), channel_id=1, source_target_pairs={{4,0},{6,2},{8,12},{10,14},{5,1},{7,3},{9,13},{11,15},{20,16},{22,... | collective-permute-start | bytes 3686408 | tf_op jit(solution)/shard_map/ppermute | solution.py:450
  463.4 99.4 %collective-permute-start.36 = (bf16[800,768]{1,0:T(8,128)(2,1)S(1)}, bf16[800,768]{1,0:T(8,128)(2,1)S(1)}, u32[]{:S(2)}, u32[]{:S(2)}) collective-permute-start(bf16[800,768]{1,0:T(8,128)(2,1)S(1)} %pad_maximum_fusion.18), channel_id=1, source_target_pairs={{16,0},{17,1},{18,2},{19,3},{20,4},{21,5},{22,6},{23,7},{24,8},{25... | collective-permute-start | bytes 3686408 | tf_op jit(solution)/shard_map/ppermute | solution.py:678
  470.3 2.8 collective-permute-start.22
  564.4 19.2 %collective-permute-start.35 = (bf16[800,768]{1,0:T(8,128)(2,1)}, bf16[800,768]{1,0:T(8,128)(2,1)}, u32[]{:S(2)}, u32[]{:S(2)}) collective-permute-start(bf16[800,768]{1,0:T(8,128)(2,1)} %get-tuple-element.141), channel_id=1, source_target_pairs={{0,16},{1,17},{2,18},{3,19},{4,20},{5,21},{6,22},{7,23},{8,24},{9,... | collective-permute-start | bytes 3686408 | tf_op jit(solution)/shard_map/ppermute | solution.py:677
  570.6 32.5 %collective-permute-start.43 = (bf16[1568,768]{1,0:T(8,128)(2,1)}, bf16[1568,768]{1,0:T(8,128)(2,1)}, u32[]{:S(2)}, u32[]{:S(2)}) collective-permute-start(bf16[1568,768]{1,0:T(8,128)(2,1)} %get-tuple-element.139), channel_id=1, source_target_pairs={{16,0},{17,1},{18,2},{19,3},{20,4},{21,5},{22,6},{23,7},{24,8},{25... | collective-permute-start | bytes 7225352 | tf_op jit(solution)/shard_map/ppermute | solution.py:678
  (46 other events, 192.4 us)
